TPU v7x, 32 devices: a whole 2x2x4 slice. The times are simulated.
32 devices in a mesh: dp: 8 (over y, x, core), tensor: 4 (over z).
Axes of the slice: x: 2, y: 2, z: 4, core: 2. Of those that a mesh axis runs over, the one named last changes fastest.
Arguments:
- hidden_in: bfloat16 [2, 4096, 2048], P(None, ('dp', 'tensor')), may hold values from -6 to 6
- out_cotangent: bfloat16 [2, 4096, 2048], P(None, ('dp', 'tensor')), may hold values from -6 to 6
- piece_start: int32 [2, 8], P(None, 'dp'), may hold values from 0 to 256, as said below
- query_weight: bfloat16 [2048, 2048], P('dp', 'tensor'), may hold values from -0.1875 to 0.1875
- key_weight: bfloat16 [2048, 2048], P('dp', 'tensor'), may hold values from -0.1875 to 0.1875
- value_weight: bfloat16 [2048, 2048], P('dp', 'tensor'), may hold values from -0.125 to 0.125
- output_weight: bfloat16 [2048, 2048], P('tensor', 'dp'), may hold values from -0.75 to 0.75
- gate_weight: bfloat16 [2048, 8192], P('dp', 'tensor'), may hold values from -0.125 to 0.125
- up_weight: bfloat16 [2048, 8192], P('dp', 'tensor'), may hold values from -0.125 to 0.125
- down_weight: bfloat16 [8192, 2048], P('tensor', 'dp'), may hold values from -0.0625 to 0.0625
- attn_gain: bfloat16 [2048], P('dp'), may hold values from 0.25 to 1.75
- mlp_gain: bfloat16 [2048], P('dp'), may hold values from 0.25 to 1.75
- memory_gate: float32 [16], P('tensor'), may hold values from -2 to 2
Outputs:
- hidden_out: bfloat16 [2, 4096, 2048], P(None, ('dp', 'tensor'))
- hidden_grad: float32 [2, 4096, 2048], P(None, ('dp', 'tensor'))
- query_weight_grad: float32 [2048, 2048], P('dp', 'tensor')
- key_weight_grad: float32 [2048, 2048], P('dp', 'tensor')
- value_weight_grad: float32 [2048, 2048], P('dp', 'tensor')
- output_weight_grad: float32 [2048, 2048], P('tensor', 'dp')
- gate_weight_grad: float32 [2048, 8192], P('dp', 'tensor')
- up_weight_grad: float32 [2048, 8192], P('dp', 'tensor')
- down_weight_grad: float32 [8192, 2048], P('tensor', 'dp')
- attn_gain_grad: float32 [2048], P('dp')
- mlp_gain_grad: float32 [2048], P('dp')
- memory_gate_grad: float32 [16], P('tensor')
Inputs may be any that keep to these rules, and one draw needn't show every extreme that they name: `piece_start`: each segment of 512 positions holds one picture piece of 256 positions, starting at this offset within the segment.
All inputs are finite; a program needn't handle non-finite values.
Results may differ from a plain program's by a relative error of at most 0.014.
The roundings to bfloat16 on the way count: a program that leaves them out, or rounds other values in their place, can miss the bound.
Values may be sent and summed in bfloat16 or wider, within the bound.
No kernel may reach another device: no remote copies, remote signals or barrier semaphores. Data moves between devices by JAX's collectives and lax.ppermute only.
A program may use at most 256 MiB of HBM per device.

v0:
```python
import jax
import jax.numpy as jnp
from jax import lax
from jax.sharding import PartitionSpec as P

HEADS = 16
HD = 128
SEG = 512
PIECE = 256


epsilon = 1e-05
highest = lax.Precision.HIGHEST


def prefix(part, axis, combine, identity):
    place = lax.axis_index(axis)
    gathered = jax.tree.map(lambda a: lax.all_gather(a, axis), part)
    state = jax.tree.map(lambda a, e: jnp.zeros_like(a) + jnp.asarray(e, a.dtype), part, identity)

    def one(hop, state):
        return combine(
            state, jax.tree.map(lambda a: lax.dynamic_index_in_dim(a, hop, 0, False), gathered)
        )

    return lax.fori_loop(0, place, one, state)


def prefix_2(array, axis, join, neutral):
    count = lax.axis_size(axis)
    place = lax.axis_index(axis)
    ahead = count - 1 - place
    gathered = jax.tree.map(
        lambda a, kind: lax.all_gather(a.astype(kind), axis),
        array,
        jax.tree.map(lambda a: jnp.bfloat16 if a.dtype == jnp.float32 else a.dtype, array),
    )
    state = jax.tree.map(lambda a, e: jnp.zeros_like(a) + jnp.asarray(e, a.dtype), array, neutral)

    def one(hop, state):
        source = count - 1 - hop
        return join(
            state,
            jax.tree.map(
                lambda a, own: lax.dynamic_index_in_dim(a, source, 0, False).astype(own.dtype),
                gathered,
                array,
            ),
        )

    return lax.fori_loop(0, ahead, one, state)


def norm_rows(values, gain_row):
    return (
        values * lax.rsqrt(jnp.mean(values * values, axis=-1, keepdims=True) + epsilon) * gain_row
    )


def elu_plus(values):
    return jnp.where(values > 0, values, jnp.expm1(jnp.minimum(values, 0.0))) + 1.0


def elu_slope(values):
    return jnp.where(values > 0, 1.0, jnp.exp(jnp.minimum(values, 0.0)))


def recall(feature_q, memory, normer):
    numerator = jnp.einsum("qhd,hde->qhe", feature_q, memory, precision=highest)
    denominator = jnp.einsum("qhd,hd->qh", feature_q, normer, precision=highest) + 1.0
    return numerator / denominator[..., None]


def carry_add(earlier_part, later_part):
    memory_a, normer_a, flag_a = earlier_part
    memory_b, normer_b, flag_b = later_part
    restart = flag_b > 0.5
    return (
        jnp.where(restart, memory_b, memory_a + memory_b),
        jnp.where(restart, normer_b, normer_a + normer_b),
        jnp.maximum(flag_a, flag_b),
    )


def contract_rows(left_side, right_side):
    return lax.dot_general(
        left_side, right_side, (((0,), (0,)), ((), ())), preferred_element_type=jnp.float32
    )


def times_transpose(left_side, right_side):
    return lax.dot_general(
        left_side, right_side, (((1,), (1,)), ((), ())), preferred_element_type=jnp.float32
    )


def spread_rows(values):
    return lax.all_gather(values, "tensor", axis=0, tiled=True)


def share_rows(values):
    return lax.psum_scatter(values, "tensor", scatter_dimension=0, tiled=True)


def spread_grads(values):
    return lax.all_gather(values, "tensor", axis=0, tiled=True)


def share_grads(values):
    return lax.psum_scatter(values, "tensor", scatter_dimension=0, tiled=True)


def score_block(query_seg, key_seg, allowed):
    scores = jnp.einsum(
        "qhd,khd->hqk", query_seg, key_seg, preferred_element_type=jnp.float32
    ) * float(HD) ** (-0.5)
    return jnp.where(allowed[None], scores, -1e30)


def add_terms(previous, current):
    if previous is None:
        return current
    return tuple((older + newer for older, newer in zip(previous, current)))


def on_device(
    hidden_in,
    out_cotangent,
    piece_start,
    query_weight,
    key_weight,
    value_weight,
    output_weight,
    gate_weight,
    up_weight,
    down_weight,
    attn_gain,
    mlp_gain,
    memory_gate,
):
    dp_index = lax.axis_index("dp")
    dp_count = lax.axis_size("dp")
    tensor_index = lax.axis_index("tensor")
    heads_here = memory_gate.shape[0]
    gain_width = attn_gain.shape[0]
    score_scale = float(HD) ** (-0.5)
    query_full, key_full, value_full, output_full, gain_one, gain_two = (
        lax.all_gather(query_weight, "dp", axis=0, tiled=True),
        lax.all_gather(key_weight, "dp", axis=0, tiled=True),
        lax.all_gather(value_weight, "dp", axis=0, tiled=True),
        lax.all_gather(output_weight, "dp", axis=1, tiled=True),
        lax.all_gather(attn_gain, "dp", axis=0, tiled=True),
        lax.all_gather(mlp_gain, "dp", axis=0, tiled=True),
    )
    gate_full, up_full, down_full = (
        lax.all_gather(gate_weight, "dp", axis=0, tiled=True),
        lax.all_gather(up_weight, "dp", axis=0, tiled=True),
        lax.all_gather(down_weight, "dp", axis=1, tiled=True),
    )
    gain_one = gain_one.astype(jnp.float32)
    gain_two = gain_two.astype(jnp.float32)
    gate_sig = jax.nn.sigmoid(memory_gate)
    mixing = gate_sig[None, :, None]
    places = jnp.arange(SEG)
    first_flag = jnp.where(dp_index == 0, 1.0, 0.0).astype(jnp.float32)
    last_flag = jnp.where(dp_index == dp_count - 1, 1.0, 0.0).astype(jnp.float32)
    keep_before = 1.0 - first_flag
    keep_after = 1.0 - last_flag
    empty_state = (
        jnp.zeros((heads_here, HD, HD), jnp.float32),
        jnp.zeros((heads_here, HD), jnp.float32),
        jnp.zeros((), jnp.float32),
    )
    mlp_totals = None
    attn_totals = None
    gain_sums = jnp.zeros((2, gain_one.shape[0]), jnp.float32)
    gate_sums = jnp.zeros((heads_here,), jnp.float32)
    outputs = []
    input_grads = []
    batch_count = hidden_in.shape[0]
    for micro_batch in range(batch_count):
        token_rows = hidden_in[micro_batch].astype(jnp.float32)
        seg_in = spread_rows(norm_rows(token_rows, gain_one).astype(jnp.bfloat16))
        query_seg = (
            jnp.dot(seg_in, query_full, preferred_element_type=jnp.float32)
            .astype(jnp.bfloat16)
            .reshape(SEG, heads_here, HD)
        )
        key_seg = (
            jnp.dot(seg_in, key_full, preferred_element_type=jnp.float32)
            .astype(jnp.bfloat16)
            .reshape(SEG, heads_here, HD)
        )
        value_seg = (
            jnp.dot(seg_in, value_full, preferred_element_type=jnp.float32)
            .astype(jnp.bfloat16)
            .reshape(SEG, heads_here, HD)
        )
        offset = piece_start[micro_batch, 0]
        inside = (places >= offset) & (places < offset + PIECE)
        allowed = (places[:, None] >= places[None, :]) | inside[:, None] & inside[None, :]
        scores = score_block(query_seg, key_seg, allowed)
        score_peak = jnp.max(scores, axis=-1, keepdims=True)
        exp_scores = jnp.exp(scores - score_peak)
        exp_total = jnp.sum(exp_scores, axis=-1, keepdims=True)
        soft_probs = exp_scores / exp_total
        log_norm = score_peak + jnp.log(exp_total)
        local_mix = jnp.einsum(
            "hqk,khd->qhd",
            soft_probs.astype(jnp.bfloat16),
            value_seg,
            preferred_element_type=jnp.float32,
        )
        query_wide = query_seg.astype(jnp.float32)
        key_wide = key_seg.astype(jnp.float32)
        value_wide = value_seg.astype(jnp.float32)
        feature_q = elu_plus(query_wide)
        feature_k = elu_plus(key_wide)
        local_mem = jnp.einsum("khd,khe->hde", feature_k, value_wide, precision=highest)
        local_nor = jnp.sum(feature_k, axis=0)
        before_mem, before_nor, unused_flag = prefix(
            (local_mem, local_nor, first_flag), "dp", carry_add, empty_state
        )
        before_mem = before_mem * keep_before
        before_nor = before_nor * keep_before
        recalled = recall(feature_q, before_mem, before_nor)
        mixture = mixing * recalled + (1.0 - mixing) * local_mix
        heads_out = mixture.reshape(SEG, heads_here * HD).astype(jnp.bfloat16)
        middle = token_rows + share_rows(
            jnp.dot(heads_out, output_full, preferred_element_type=jnp.float32)
        )
        seg_two = spread_rows(norm_rows(middle, gain_two).astype(jnp.bfloat16))
        gated = jnp.dot(seg_two, gate_full, preferred_element_type=jnp.float32)
        upper = jnp.dot(seg_two, up_full, preferred_element_type=jnp.float32)
        gated_sig = jax.nn.sigmoid(gated)
        hidden_act = (gated * gated_sig * upper).astype(jnp.bfloat16)
        mlp_rows = share_rows(jnp.dot(hidden_act, down_full, preferred_element_type=jnp.float32))
        outputs.append((middle + mlp_rows).astype(jnp.bfloat16))
        cot_rows = out_cotangent[micro_batch]
        cot_seg = spread_grads(cot_rows)
        act_grad = times_transpose(cot_seg, down_full)
        term_down = contract_rows(hidden_act, cot_seg)
        gated_grad = (act_grad * upper * gated_sig * (1.0 + gated * (1.0 - gated_sig))).astype(
            jnp.bfloat16
        )
        upper_grad = (act_grad * gated * gated_sig).astype(jnp.bfloat16)
        term_gate = contract_rows(seg_two, gated_grad)
        term_up = contract_rows(seg_two, upper_grad)
        mlp_totals = add_terms(mlp_totals, (term_gate, term_up, term_down))
        mid_norm_grad = share_grads(
            times_transpose(gated_grad, gate_full) + times_transpose(upper_grad, up_full)
        )
        unused_out, pull_two = jax.vjp(norm_rows, middle, gain_two)
        middle_norm_grad, gain_two_term = pull_two(mid_norm_grad)
        middle_grad = cot_rows.astype(jnp.float32) + middle_norm_grad
        mid_seg = spread_grads(middle_grad.astype(jnp.bfloat16))
        mixture_grad = times_transpose(mid_seg, output_full).reshape(SEG, heads_here, HD)
        term_out = contract_rows(heads_out, mid_seg)
        gate_sums = gate_sums + jnp.sum(
            mixture_grad * (recalled - local_mix), axis=(0, 2)
        ) * gate_sig * (1.0 - gate_sig)
        local_grad = ((1.0 - mixing) * mixture_grad).astype(jnp.bfloat16)
        recall_grad = mixing * mixture_grad
        soft_again = jnp.exp(score_block(query_seg, key_seg, allowed) - log_norm)
        value_grad = jnp.einsum(
            "hqk,qhd->khd",
            soft_again.astype(jnp.bfloat16),
            local_grad,
            preferred_element_type=jnp.float32,
        )
        prob_grad = jnp.einsum(
            "qhd,khd->hqk", local_grad, value_seg, preferred_element_type=jnp.float32
        )
        row_delta = jnp.sum(soft_again * prob_grad, axis=-1, keepdims=True)
        score_grad = (soft_again * (prob_grad - row_delta)).astype(jnp.bfloat16)
        query_grad = (
            jnp.einsum("hqk,khd->qhd", score_grad, key_seg, preferred_element_type=jnp.float32)
            * score_scale
        )
        key_grad = (
            jnp.einsum("hqk,qhd->khd", score_grad, query_seg, preferred_element_type=jnp.float32)
            * score_scale
        )
        unused_recall, pull_recall = jax.vjp(recall, feature_q, before_mem, before_nor)
        feature_q_grad, mem_grad, nor_grad = pull_recall(recall_grad)
        mem_grad = mem_grad * keep_before
        nor_grad = nor_grad * keep_before
        after_mem, after_nor, unused_flag = prefix_2(
            (mem_grad, nor_grad, last_flag), "dp", carry_add, empty_state
        )
        after_mem = after_mem * keep_after
        after_nor = after_nor * keep_after
        feature_k_grad = (
            jnp.einsum("khe,hde->khd", value_wide, after_mem, precision=highest) + after_nor[None]
        )
        value_grad = value_grad + jnp.einsum(
            "khd,hde->khe", feature_k, after_mem, precision=highest
        )
        query_low = (
            (query_grad + feature_q_grad * elu_slope(query_wide))
            .astype(jnp.bfloat16)
            .reshape(SEG, heads_here * HD)
        )
        key_low = (
            (key_grad + feature_k_grad * elu_slope(key_wide))
            .astype(jnp.bfloat16)
            .reshape(SEG, heads_here * HD)
        )
        value_low = value_grad.astype(jnp.bfloat16).reshape(SEG, heads_here * HD)
        term_query = contract_rows(seg_in, query_low)
        term_key = contract_rows(seg_in, key_low)
        term_value = contract_rows(seg_in, value_low)
        attn_totals = add_terms(attn_totals, (term_query, term_key, term_value, term_out))
        in_norm_grad = share_grads(
            times_transpose(query_low, query_full)
            + times_transpose(key_low, key_full)
            + times_transpose(value_low, value_full)
        )
        unused_norm, pull_one = jax.vjp(norm_rows, token_rows, gain_one)
        input_norm_grad, gain_one_term = pull_one(in_norm_grad)
        input_grads.append(middle_grad + input_norm_grad)
        gain_sums = gain_sums + jnp.stack([gain_one_term, gain_two_term])
    totals = (
        lax.psum_scatter(attn_totals[0], "dp", scatter_dimension=0, tiled=True),
        lax.psum_scatter(attn_totals[1], "dp", scatter_dimension=0, tiled=True),
        lax.psum_scatter(attn_totals[2], "dp", scatter_dimension=0, tiled=True),
        lax.psum_scatter(attn_totals[3], "dp", scatter_dimension=1, tiled=True),
        lax.psum_scatter(mlp_totals[0], "dp", scatter_dimension=0, tiled=True),
        lax.psum_scatter(mlp_totals[1], "dp", scatter_dimension=0, tiled=True),
        lax.psum_scatter(mlp_totals[2], "dp", scatter_dimension=1, tiled=True),
    )
    placed = lax.dynamic_update_slice(
        jnp.zeros((HEADS,), jnp.float32), gate_sums, (tensor_index * heads_here,)
    )
    gain_total, gate_total = lax.psum((gain_sums, placed), ("dp", "tensor"))
    attn_gain_grad = lax.dynamic_slice_in_dim(gain_total[0], dp_index * gain_width, gain_width)
    mlp_gain_grad = lax.dynamic_slice_in_dim(gain_total[1], dp_index * gain_width, gain_width)
    memory_gate_grad = lax.dynamic_slice_in_dim(gate_total, tensor_index * heads_here, heads_here)
    return (
        jnp.stack(outputs),
        jnp.stack(input_grads),
        totals[0],
        totals[1],
        totals[2],
        totals[3],
        totals[4],
        totals[5],
        totals[6],
        attn_gain_grad,
        mlp_gain_grad,
        memory_gate_grad,
    )


def solution(mesh):
    placed = (
        P(None, ("dp", "tensor"), None),
        P(None, ("dp", "tensor"), None),
        P(None, "dp"),
        P("dp", "tensor"),
        P("dp", "tensor"),
        P("dp", "tensor"),
        P("tensor", "dp"),
        P("dp", "tensor"),
        P("dp", "tensor"),
        P("tensor", "dp"),
        P("dp"),
        P("dp"),
        P("tensor"),
    )
    return jax.shard_map(
        on_device,
        mesh=mesh,
        in_specs=placed,
        out_specs=(
            P(None, ("dp", "tensor"), None),
            P(None, ("dp", "tensor"), None),
            P("dp", "tensor"),
            P("dp", "tensor"),
            P("dp", "tensor"),
            P("tensor", "dp"),
            P("dp", "tensor"),
            P("dp", "tensor"),
            P("tensor", "dp"),
            P("dp"),
            P("dp"),
            P("tensor"),
        ),
        check_vma=False,
    )
```

profile of v0, /device:TPU:0, one launch (start us, length us, event | category | flops | bytes accessed | tf_op | source)
XLA Modules:
  0.0 2087.8 jit_solution(16399876243666384445)
XLA Ops:
  25.5 43.7 %all-gather.32.cloned.1.call-done = bf16[512,2048]{1,0:T(8,128)(2,1)} async-done(((bf16[128,2048]{1,0:T(8,128)(2,1)}), bf16[512,2048]{1,0:T(8,128)(2,1)}) %all-gather.32.cloned.1.call-update) | async-done | bytes 2097168 | tf_op jit(solution)/shard_map/all_gather | solution.py:98
  132.8 42.8 %all-gather.50.cloned.1.call-done = bf16[512,2048]{1,0:T(8,128)(2,1)} async-done(((bf16[128,2048]{1,0:T(8,128)(2,1)}), bf16[512,2048]{1,0:T(8,128)(2,1)}) %all-gather.50.cloned.1.call-update) | async-done | bytes 2097168 | tf_op jit(solution)/shard_map/all_gather | solution.py:98
  312.9 63.8 %reduce-scatter.16.cloned.1.call-done = f32[128,2048]{1,0:T(8,128)} async-done(((f32[512,2048]{1,0:T(8,128)}), f32[128,2048]{1,0:T(8,128)}) %reduce-scatter.16.cloned.1.call-update) | async-done | bytes 1048592 | tf_op jit(solution)/shard_map/reduce_scatter | solution.py:102
  376.7 79.6 %reduce-scatter.20.cloned.1.call-done = f32[128,2048]{1,0:T(8,128)} async-done(((f32[512,2048]{1,0:T(8,128)}), f32[128,2048]{1,0:T(8,128)}) %reduce-scatter.20.cloned.1.call-update) | async-done | bytes 1048592 | tf_op jit(solution)/shard_map/reduce_scatter | solution.py:102
  463.3 49.7 %all-gather.44.cloned.1.call-done = bf16[2048,2048]{1,0:T(8,128)(2,1)} async-done(((bf16[256,2048]{1,0:T(8,128)(2,1)}), bf16[2048,2048]{1,0:T(8,128)(2,1)}) %all-gather.44.cloned.1.call-update) | async-done | bytes 8388624 | tf_op jit(solution)/shard_map/all_gather | solution.py:156
  513.1 48.0 %all-gather.42.cloned.1.call-done = bf16[512,2048]{1,0:T(8,128)(2,1)} async-done(((bf16[128,2048]{1,0:T(8,128)(2,1)}), bf16[512,2048]{1,0:T(8,128)(2,1)}) %all-gather.42.cloned.1.call-update) | async-done | bytes 2097168 | tf_op jit(solution)/shard_map/all_gather | solution.py:98
  571.5 44.6 %all-gather.46.cloned.1.call-done = bf16[2048,2048]{1,0:T(8,128)(2,1)} async-done(((bf16[256,2048]{1,0:T(8,128)(2,1)}), bf16[2048,2048]{1,0:T(8,128)(2,1)}) %all-gather.46.cloned.1.call-update) | async-done | bytes 8388624 | tf_op jit(solution)/shard_map/all_gather | solution.py:157
  626.6 37.5 %all-gather.62.cloned.1.call-done = bf16[1,512,2048]{2,1,0:T(8,128)(2,1)} async-done(((bf16[1,128,2048]{2,1,0:T(8,128)(2,1)}), bf16[1,512,2048]{2,1,0:T(8,128)(2,1)}) %all-gather.62.cloned.1.call-update) | async-done | bytes 2097168 | tf_op jit(solution)/shard_map/all_gather | solution.py:106
  664.0 56.4 %all-gather.48.cloned.1.call-done = bf16[2048,2048]{1,0:T(8,128)(2,1)} async-done(((bf16[2048,256]{1,0:T(8,128)(2,1)}), bf16[2048,2048]{1,0:T(8,128)(2,1)}) %all-gather.48.cloned.1.call-update) | async-done | bytes 8388624 | tf_op jit(solution)/shard_map/all_gather | solution.py:158
  747.6 76.8 %reduce-scatter.24.cloned.1.call-done = f32[128,2048]{1,0:T(8,128)} async-done(((f32[512,2048]{1,0:T(8,128)}), f32[128,2048]{1,0:T(8,128)}) %reduce-scatter.24.cloned.1.call-update) | async-done | bytes 1048592 | tf_op jit(solution)/shard_map/reduce_scatter | solution.py:110
  828.0 46.0 %all-gather.52.cloned.1.call-done = bf16[512,2048]{1,0:T(8,128)(2,1)} async-done(((bf16[128,2048]{1,0:T(8,128)(2,1)}), bf16[512,2048]{1,0:T(8,128)(2,1)}) %all-gather.52.cloned.1.call-update) | async-done | bytes 2097168 | tf_op jit(solution)/shard_map/all_gather | solution.py:98
  961.5 64.8 %reduce-scatter.28.cloned.1.call-done = f32[128,2048]{1,0:T(8,128)} async-done(((f32[512,2048]{1,0:T(8,128)}), f32[128,2048]{1,0:T(8,128)}) %reduce-scatter.28.cloned.1.call-update) | async-done | bytes 1048592 | tf_op jit(solution)/shard_map/reduce_scatter | solution.py:110
  1028.3 77.4 %reduce-scatter.22.cloned.1.call-done = f32[128,2048]{1,0:T(8,128)} async-done(((f32[512,2048]{1,0:T(8,128)}), f32[128,2048]{1,0:T(8,128)}) %reduce-scatter.22.cloned.1.call-update) | async-done | bytes 1048592 | tf_op jit(solution)/shard_map/reduce_scatter | solution.py:102
  1124.6 31.3 %all-gather.54.cloned.1.call-done = bf16[512,2048]{1,0:T(8,128)(2,1)} async-done(((bf16[128,2048]{1,0:T(8,128)(2,1)}), bf16[512,2048]{1,0:T(8,128)(2,1)}) %all-gather.54.cloned.1.call-update) | async-done | bytes 2097168 | tf_op jit(solution)/shard_map/all_gather | solution.py:106
  1167.3 35.0 %all-gather.56.cloned.1.call-done = bf16[512,2048]{1,0:T(8,128)(2,1)} async-done(((bf16[128,2048]{1,0:T(8,128)(2,1)}), bf16[512,2048]{1,0:T(8,128)(2,1)}) %all-gather.56.cloned.1.call-update) | async-done | bytes 2097168 | tf_op jit(solution)/shard_map/all_gather | solution.py:106
  1422.6 43.4 %all-reduce.2 = (f32[2,2048]{1,0:T(2,128)S(1)}, f32[16]{0:T(128)S(1)}) all-reduce(f32[2,2048]{1,0:T(2,128)S(1)} %maximum_add_fusion, f32[16]{0:T(128)S(1)} %fusion.171), channel_id=1, replica_groups=mesh['dp'=8,'tensor'=4] {'dp','tensor'}, use_global_device_ids=true, to_apply=%region_45.46 | all-reduce | flops 4112 | bytes 32896 | tf_op jit(solution)/shard_map/psum | solution.py:335
  1467.2 30.9 %reduce-scatter.18.cloned.1.call-done = f32[128,2048]{1,0:T(8,128)} async-done(((f32[512,2048]{1,0:T(8,128)}), f32[128,2048]{1,0:T(8,128)}) %reduce-scatter.18.cloned.1.call-update) | async-done | bytes 1048592 | tf_op jit(solution)/shard_map/reduce_scatter | solution.py:102
  1504.0 49.9 %reduce-scatter.32.cloned.1.call-done = f32[256,512]{1,0:T(8,128)} async-done(((f32[2048,512]{1,0:T(8,128)}), f32[256,512]{1,0:T(8,128)}) %reduce-scatter.32.cloned.1.call-update) | async-done | bytes 524304 | tf_op jit(solution)/shard_map/reduce_scatter | solution.py:324
  1553.9 55.7 %reduce-scatter.38.cloned.1.call-done = f32[512,256]{1,0:T(8,128)} async-done(((f32[512,2048]{1,0:T(8,128)}), f32[512,256]{1,0:T(8,128)}) %reduce-scatter.38.cloned.1.call-update) | async-done | bytes 524304 | tf_op jit(solution)/shard_map/reduce_scatter | solution.py:327
  1609.6 55.1 %reduce-scatter.34.cloned.1.call-done = f32[256,512]{1,0:T(8,128)} async-done(((f32[2048,512]{1,0:T(8,128)}), f32[256,512]{1,0:T(8,128)}) %reduce-scatter.34.cloned.1.call-update) | async-done | bytes 524304 | tf_op jit(solution)/shard_map/reduce_scatter | solution.py:325
  1664.7 55.7 %reduce-scatter.36.cloned.1.call-done = f32[256,512]{1,0:T(8,128)} async-done(((f32[2048,512]{1,0:T(8,128)}), f32[256,512]{1,0:T(8,128)}) %reduce-scatter.36.cloned.1.call-update) | async-done | bytes 524304 | tf_op jit(solution)/shard_map/reduce_scatter | solution.py:326
  1720.4 120.1 %reduce-scatter.40.cloned.1.call-done = f32[256,2048]{1,0:T(8,128)} async-done(((f32[2048,2048]{1,0:T(8,128)}), f32[256,2048]{1,0:T(8,128)}) %reduce-scatter.40.cloned.1.call-update) | async-done | bytes 2097168 | tf_op jit(solution)/shard_map/reduce_scatter | solution.py:328
  1840.5 120.0 %reduce-scatter.42.cloned.1.call-done = f32[256,2048]{1,0:T(8,128)} async-done(((f32[2048,2048]{1,0:T(8,128)}), f32[256,2048]{1,0:T(8,128)}) %reduce-scatter.42.cloned.1.call-update) | async-done | bytes 2097168 | tf_op jit(solution)/shard_map/reduce_scatter | solution.py:329
  1960.5 120.2 %reduce-scatter.44.cloned.1.call-done = f32[2048,256]{1,0:T(8,128)} async-done(((f32[2048,2048]{1,0:T(8,128)}), f32[2048,256]{1,0:T(8,128)}) %reduce-scatter.44.cloned.1.call-update) | async-done | bytes 2097168 | tf_op jit(solution)/shard_map/reduce_scatter | solution.py:330
  (513 shorter events, 644.8 us)
Async XLA Ops:
  24.3 151.2 %all-gather.50.cloned.1.call-start = ((), (), s32[]{:S(2)}) async-start(), calls=%async_computation.26 | async-start | bytes 2621440 | tf_op jit(solution)/shard_map/all_gather | solution.py:98
  24.9 188.2 %all-gather.38.cloned.1.call-start = ((), (), s32[]{:S(2)}) async-start(), calls=%async_computation.18 | async-start | bytes 2359296 | tf_op jit(solution)/shard_map/all_gather | solution.py:148
  25.5 208.7 %all-gather.58.cloned.1.call-start = ((), (), s32[]{:S(2)}) async-start(), calls=%async_computation.43 | async-start | bytes 2359296 | tf_op jit(solution)/shard_map/all_gather | solution.py:18
  185.4 191.3 %reduce-scatter.16.cloned.1.call-start = ((), (), s32[]{:S(2)}) async-start(), calls=%async_computation.20 | async-start | bytes 5242880 | tf_op jit(solution)/shard_map/reduce_scatter | solution.py:102
  299.8 156.5 %reduce-scatter.20.cloned.1.call-start = ((), (), s32[]{:S(2)}) async-start(), calls=%async_computation.27 | async-start | bytes 5242880 | tf_op jit(solution)/shard_map/reduce_scatter | solution.py:102
  303.2 209.9 %all-gather.44.cloned.1.call-start = ((), (), s32[]{:S(2)}) async-start(), calls=%async_computation.22 | async-start | bytes 9437184 | tf_op jit(solution)/shard_map/all_gather | solution.py:156
  303.9 257.1 %all-gather.42.cloned.1.call-start = ((), (), s32[]{:S(2)}) async-start(), calls=%async_computation.21 | async-start | bytes 2621440 | tf_op jit(solution)/shard_map/all_gather | solution.py:98
  459.3 156.7 %all-gather.46.cloned.1.call-start = ((), (), s32[]{:S(2)}) async-start(), calls=%async_computation.23 | async-start | bytes 9437184 | tf_op jit(solution)/shard_map/all_gather | solution.py:157
  460.1 203.9 %all-gather.62.cloned.1.call-start = ((), (), s32[]{:S(2)}) async-start(), calls=%async_computation.45 | async-start | bytes 2621440 | tf_op jit(solution)/shard_map/all_gather | solution.py:106
  462.4 258.0 %all-gather.48.cloned.1.call-start = ((), (), s32[]{:S(2)}) async-start(), calls=%async_computation.24 | async-start | bytes 9437184 | tf_op jit(solution)/shard_map/all_gather | solution.py:158
  463.0 361.4 %reduce-scatter.24.cloned.1.call-start = ((), (), s32[]{:S(2)}) async-start(), calls=%async_computation.30 | async-start | bytes 5242880 | tf_op jit(solution)/shard_map/reduce_scatter | solution.py:110
  827.9 198.3 %reduce-scatter.28.cloned.1.call-start = ((), (), s32[]{:S(2)}) async-start(), calls=%async_computation.33 | async-start | bytes 5242880 | tf_op jit(solution)/shard_map/reduce_scatter | solution.py:110
  950.6 155.1 %reduce-scatter.22.cloned.1.call-start = ((), (), s32[]{:S(2)}) async-start(), calls=%async_computation.29 | async-start | bytes 5242880 | tf_op jit(solution)/shard_map/reduce_scatter | solution.py:102
  961.2 194.8 %all-gather.54.cloned.1.call-start = ((), (), s32[]{:S(2)}) async-start(), calls=%async_computation.31 | async-start | bytes 2621440 | tf_op jit(solution)/shard_map/all_gather | solution.py:106
  1229.1 190.6 %reduce-scatter.26.cloned.1.call-start = ((), (), s32[]{:S(2)}) async-start(), calls=%async_computation.32 | async-start | bytes 5242880 | tf_op jit(solution)/shard_map/reduce_scatter | solution.py:110
  1264.5 155.3 %reduce-scatter.30.cloned.1.call-start = ((), (), s32[]{:S(2)}) async-start(), calls=%async_computation.35 | async-start | bytes 5242880 | tf_op jit(solution)/shard_map/reduce_scatter | solution.py:110
  1317.0 181.1 %reduce-scatter.18.cloned.1.call-start = ((), (), s32[]{:S(2)}) async-start(), calls=%async_computation.25 | async-start | bytes 5242880 | tf_op jit(solution)/shard_map/reduce_scatter | solution.py:102
  1328.1 225.8 %reduce-scatter.32.cloned.1.call-start = ((), (), s32[]{:S(2)}) async-start(), calls=%async_computation.36 | async-start | bytes 4718592 | tf_op jit(solution)/shard_map/reduce_scatter | solution.py:324
  1335.5 274.1 %reduce-scatter.38.cloned.1.call-start = ((), (), s32[]{:S(2)}) async-start(), calls=%async_computation.39 | async-start | bytes 4718592 | tf_op jit(solution)/shard_map/reduce_scatter | solution.py:327
  1342.8 321.9 %reduce-scatter.34.cloned.1.call-start = ((), (), s32[]{:S(2)}) async-start(), calls=%async_computation.37 | async-start | bytes 4718592 | tf_op jit(solution)/shard_map/reduce_scatter | solution.py:325
  1350.2 370.2 %reduce-scatter.36.cloned.1.call-start = ((), (), s32[]{:S(2)}) async-start(), calls=%async_computation.38 | async-start | bytes 4718592 | tf_op jit(solution)/shard_map/reduce_scatter | solution.py:326
  1357.7 482.9 %reduce-scatter.40.cloned.1.call-start = ((), (), s32[]{:S(2)}) async-start(), calls=%async_computation.40 | async-start | bytes 18874368 | tf_op jit(solution)/shard_map/reduce_scatter | solution.py:328
  1378.3 582.3 %reduce-scatter.42.cloned.1.call-start = ((), (), s32[]{:S(2)}) async-start(), calls=%async_computation.41 | async-start | bytes 18874368 | tf_op jit(solution)/shard_map/reduce_scatter | solution.py:329
  1398.6 682.1 %reduce-scatter.44.cloned.1.call-start = ((), (), s32[]{:S(2)}) async-start(), calls=%async_computation.42 | async-start | bytes 18874368 | tf_op jit(solution)/shard_map/reduce_scatter | solution.py:330
  (131 other events, 5919.4 us)
Sparse Core Ops, SparseCore 0:
  23.0 46.2 all-gather.31
  129.6 45.9 all-gather.49
  299.9 76.7 reduce-scatter.15
  378.9 77.2 reduce-scatter.19
  458.1 54.8 all-gather.43
  515.1 45.9 all-gather.41
  562.9 53.0 all-gather.45
  618.1 45.9 all-gather.61
  665.7 54.6 all-gather.47
  747.6 76.7 reduce-scatter.23
  827.5 46.4 all-gather.51
  950.7 75.4 reduce-scatter.27
  1028.4 77.2 reduce-scatter.21
  1109.5 46.4 all-gather.53
  1264.6 73.5 reduce-scatter.25
  1340.3 77.2 reduce-scatter.29
  1419.8 78.3 reduce-scatter.17
  1502.1 51.7 reduce-scatter.31
  1558.2 51.3 reduce-scatter.37
  1613.4 51.2 reduce-scatter.33
  1669.0 51.3 reduce-scatter.35
  1724.6 115.9 reduce-scatter.39
  1844.5 115.9 reduce-scatter.41
  1964.7 115.9 reduce-scatter.43
  (10 shorter events, 299.5 us)
where the time goes:
time: 2100 us; the launch traced here: 2090 us
  waiting for transfers between devices  1550 us (74%)
  matrix products  304 us (14%)
  blocking collectives  123 us (6%)
  other arithmetic  49 us (2%)
  local copies, waits for them, and re-layouts  35.6 us (2%)
    reduce_scatter x4, waiting for transfers between devices, share_rows(): return lax.psum_scatter(values, 'tensor', scatter_dimension=0, tiled=True)  252 us
    all_gather x4, waiting for transfers between devices, spread_rows(): return lax.all_gather(values, 'tensor', axis=0, tiled=True)  180 us
    reduce_scatter x4, waiting for transfers between devices, share_grads(): return lax.psum_scatter(values, 'tensor', scatter_dimension=0, tiled=True)  142 us
    all_gather x4, waiting for transfers between devices, spread_grads(): return lax.all_gather(values, 'tensor', axis=0, tiled=True)  130 us
    reduce_scatter x1, waiting for transfers between devices, on_device(): lax.psum_scatter(mlp_totals[2], 'dp', scatter_dimension=1, tiled=True)  120 us
    reduce_scatter x1, waiting for transfers between devices, on_device(): lax.psum_scatter(mlp_totals[0], 'dp', scatter_dimension=0, tiled=True)  120 us
    reduce_scatter x1, waiting for transfers between devices, on_device(): lax.psum_scatter(mlp_totals[1], 'dp', scatter_dimension=0, tiled=True)  120 us
    dot_general x14, matrix products, contract_rows(): lax.dot_general(left_side, right_side, (((0,), (0,)), ((), ())), preferre...  85.7 us
  transfers between devices with their start and end apart: 34, of which 29 were waited for; matrix products, arithmetic and copies ran while one was open for 14% of the time, Pallas kernels for 0%

commit v1 on v0

v1 whole, which is shorter than its diff:
```python
import functools
from types import SimpleNamespace

import jax
import jax.numpy as jnp
from jax import lax
from jax.experimental import pallas as pl
from jax.experimental.pallas import tpu as pltpu
from jax.sharding import PartitionSpec as P

HD = 128
PIECE = 256
epsilon = 1e-05
highest = lax.Precision.HIGHEST
bf16 = jnp.bfloat16
f32 = jnp.float32


class Order:
    def __init__(self):
        self.last = None

    def place(self, values):
        if self.last is None:
            return values
        return lax.optimization_barrier((values, self.last))[0]

    def done(self, values):
        self.last = values
        return values


NEAR = [(0, 0), (0, 1), (2, 1), (2, 0), (6, 0), (6, 1), (4, 1), (4, 0)]


def far_bits(count):
    bits = [1]
    while 2 ** (2 + len(bits)) < count:
        bits.append(2 ** (2 + len(bits)))
    return bits


def half_order(count):
    order = list(NEAR)
    for bit in far_bits(count):
        order = order + [(offset | bit, half) for offset, half in order]
    return order


def flip(values, bit):
    count = lax.axis_size("dp")
    return lax.ppermute(values, "dp", [(i, i ^ bit) for i in range(count)])


def cut(values, parts, axis):
    size = values.shape[axis] // parts
    return [lax.slice_in_dim(values, k * size, (k + 1) * size, axis=axis) for k in range(parts)]


def join_kernel(axis, own_ref, a_ref, b_ref, far_0_ref, far_1_ref, out_ref):
    size = far_0_ref.shape[axis]

    def part(ref, place, count=1):
        where = slice(place * size, (place + count) * size)
        return (where, slice(None)) if axis == 0 else (slice(None), where)

    out_ref[part(out_ref, 0, 2)] = own_ref[...]
    out_ref[part(out_ref, 2)] = a_ref[part(a_ref, 1)]
    out_ref[part(out_ref, 3)] = a_ref[part(a_ref, 0)]
    out_ref[part(out_ref, 4)] = far_0_ref[...]
    out_ref[part(out_ref, 5)] = far_1_ref[...]
    out_ref[part(out_ref, 6)] = b_ref[part(b_ref, 1)]
    out_ref[part(out_ref, 7)] = b_ref[part(b_ref, 0)]


def join_blocks(own, near_a, near_b, far_0, far_1, axis):
    if axis == 1 and far_0.shape[1] % HD:
        a, b = cut(near_a, 2, axis), cut(near_b, 2, axis)
        return jnp.concatenate([own, a[1], a[0], far_0, far_1, b[1], b[0]], axis=axis)
    other = 1 - axis
    parts = 4 if own.shape[other] % (4 * HD) == 0 else 1
    shape = list(own.shape)
    shape[axis] *= 4

    def block(dims):
        dims = list(dims)
        dims[other] //= parts
        return pl.BlockSpec(tuple(dims), lambda j: (0, j) if axis == 0 else (j, 0))

    arrays = (own, near_a, near_b, far_0, far_1)
    return pl.pallas_call(
        functools.partial(join_kernel, axis),
        grid=(parts,),
        in_specs=[block(array.shape) for array in arrays],
        out_specs=block(shape),
        out_shape=jax.ShapeDtypeStruct(tuple(shape), own.dtype),
        compiler_params=params(),
        cost_estimate=cost(64, 64),
    )(*arrays)


class Spread:
    def __init__(self, order, own, axis):
        self.order, self.axis = order, axis
        self.own = order.place(own)
        self.near_a, self.near_b = flip(self.own, 2), flip(self.own, 4)

    def second(self):
        self.near_a, self.near_b = self.order.done(self.order.place((self.near_a, self.near_b)))
        b_0 = cut(self.near_b, 2, self.axis)[0]
        a_1 = cut(self.near_a, 2, self.axis)[1]
        self.far = flip(b_0, 2), flip(a_1, 4)

    def third(self):
        far = self.order.place(self.far)
        known = self.order.done(join_blocks(self.own, self.near_a, self.near_b, *far, self.axis))
        bits = far_bits(lax.axis_size("dp"))
        for bit in bits[:-1]:
            known = jnp.concatenate([known, flip(known, bit)], axis=self.axis)
        self.whole = known, flip(known, bits[-1])

    def arrive(self):
        self.whole = self.order.done(self.order.place(self.whole))


def plus(*terms):
    total = terms[0].astype(f32)
    for term in terms[1:]:
        total = total + term.astype(f32)
    return total


class Collect:
    def __init__(self, order, product, axis):
        self.order, self.product, self.axis = order, product, axis
        self.bits = far_bits(lax.axis_size("dp"))
        product_two = order.done(product(1))
        self.received = flip(product_two, self.bits[-1])

    def second(self):
        total = self.order.done(self.product(0, self.received))
        axis = self.axis
        for bit in reversed(self.bits[:-1]):
            one, two = cut(total, 2, axis)
            total = plus(one, flip(two, bit)).astype(bf16)
        self.parts = cut(total, 8, axis)
        size = self.parts[0].shape[axis]
        self.got_x = flip(lax.slice_in_dim(total, 3 * size, 5 * size, axis=axis), 2)
        self.got_y = flip(lax.slice_in_dim(total, 5 * size, 7 * size, axis=axis), 4)

    def third(self):
        got_x, got_y = self.order.place((self.got_x, self.got_y))
        self.mine_x, pass_x = cut(got_x, 2, self.axis)
        pass_y, self.mine_y = cut(got_y, 2, self.axis)
        go_x = plus(self.parts[2], pass_y).astype(bf16)
        go_y = plus(self.parts[7], pass_x).astype(bf16)
        go_x, go_y = self.order.done((go_x, go_y))
        self.last_x, self.last_y = flip(go_x, 2), flip(go_y, 4)

    def finish(self):
        self.last_x, self.last_y = self.order.place((self.last_x, self.last_y))
        return self.order.done(
            jnp.concatenate(
                [
                    plus(self.parts[0], self.mine_x, self.last_y),
                    plus(self.parts[1], self.last_x, self.mine_y),
                ],
                axis=self.axis,
            )
        )


def move_kernel(table_ref, *refs):
    count = len(refs) // 2
    pieces = table_ref.shape[0]
    width = refs[0].shape[-1] // pieces
    for source, target in zip(refs[:count], refs[count:]):
        for k in range(pieces):
            start = pl.multiple_of(table_ref[k] * width, width)
            target[..., k * width : (k + 1) * width] = source[..., pl.ds(start, width)]


def move_columns(arrays, table):
    width = arrays[0].shape[-1] // table.shape[0]
    if width % HD:
        return [
            jnp.concatenate(
                [
                    lax.dynamic_slice_in_dim(values, table[k] * width, width, axis=-1)
                    for k in range(table.shape[0])
                ],
                axis=-1,
            )
            for values in arrays
        ]
    vmem = pl.BlockSpec(memory_space=pltpu.VMEM)
    return pl.pallas_call(
        move_kernel,
        in_specs=[pl.BlockSpec(memory_space=pltpu.SMEM)] + [vmem for _ in arrays],
        out_specs=[vmem for _ in arrays],
        out_shape=[jax.ShapeDtypeStruct(values.shape, values.dtype) for values in arrays],
        compiler_params=pltpu.CompilerParams(vmem_limit_bytes=24 * 1024 * 1024),
    )(table, *arrays)


def tables(place, order):
    count = len(order) // 2
    inward = [[(own ^ offset) * 2 + half for offset, half in order] for own in range(count)]
    outward = [[row.index(block) for block in range(2 * count)] for row in inward]
    return [
        lax.dynamic_index_in_dim(jnp.asarray(table, jnp.int32), place, 0, False)
        for table in (inward, outward)
    ]


PAIRS = [(0, 1), (1, 0), (2, 3), (3, 2)]
MIDDLE = [(1, 2), (2, 1)]
OUTER = [(1, 0), (2, 3)]
INNER = [(0, 1), (3, 2)]


def send(values, pairs):
    return lax.ppermute(values, "tensor", pairs)


def at_end():
    place = lax.axis_index("tensor")
    return (place == 0) | (place == 3)


def slot_owner():
    place = lax.axis_index("tensor")
    low = place < 2
    return [place, place ^ 1, jnp.where(low, 2, 1), jnp.where(low, 3, 0)]


def offload_gather(own):
    return lax.all_gather(own, "tensor", axis=0, tiled=True)


class OffloadGather:
    def __init__(self, order, own):
        self.order = order
        self.whole = offload_gather(order.place(own))

    def finish(self):
        return self.whole


class OffloadScatter:
    def __init__(self, order, values):
        self.order = order
        self.own = lax.psum_scatter(values, "tensor", scatter_dimension=0, tiled=True)

    def finish(self):
        return self.order.place(self.own).astype(f32)


class Gather:
    def __init__(self, order, own):
        self.order = order
        self.own = order.place(own)
        self.partner = send(self.own, PAIRS)
        self.middle_near = send(self.own, MIDDLE)

    def second(self):
        self.partner, self.middle_near = self.order.done(
            self.order.place((self.partner, self.middle_near))
        )
        self.middle_far = send(self.partner, MIDDLE)
        self.outer_near = send(self.middle_near, OUTER)

    def third(self):
        self.middle_far, self.outer_near = self.order.done(
            self.order.place((self.middle_far, self.outer_near))
        )
        self.outer_far = send(self.middle_far, OUTER)

    def finish(self):
        outer_far = self.order.place(self.outer_far)
        end = at_end()
        near = jnp.where(end, self.outer_near, self.middle_near)
        far = jnp.where(end, outer_far, self.middle_far)
        rows = self.own.shape[0]
        whole = jnp.zeros((4 * rows, self.own.shape[1]), self.own.dtype)
        for owner, piece in zip(slot_owner(), (self.own, self.partner, near, far)):
            whole = lax.dynamic_update_slice_in_dim(whole, piece, owner * rows, axis=0)
        return self.order.done(whole)


class Scatter:
    def __init__(self, order, values):
        rows = values.shape[0] // 4
        self.order = order
        self.own, self.partner, self.near, self.far = [
            lax.dynamic_slice_in_dim(values, owner * rows, rows, axis=0) for owner in slot_owner()
        ]
        self.inner_far = send(self.far, INNER)
        self.inner_near = send(self.near, INNER)

    def second(self):
        go = self.order.done(plus(self.far, self.order.place(self.inner_far)).astype(bf16))
        self.middle_far = send(go, MIDDLE)

    def third(self):
        inner_near, middle_far = self.order.place((self.inner_near, self.middle_far))
        go_near = plus(self.near, inner_near).astype(bf16)
        go_pair = plus(self.partner, middle_far).astype(bf16)
        go_near, go_pair = self.order.done((go_near, go_pair))
        self.paired = send(go_pair, PAIRS)
        self.middle_near = send(go_near, MIDDLE)

    def finish(self):
        paired, middle_near = self.order.place((self.paired, self.middle_near))
        return plus(self.own, paired, middle_near)


class Scan:
    def __init__(self, order, memory, normer, later):
        self.order, self.later = order, later
        self.heads = normer.shape[0]
        self.total = jnp.concatenate(
            [memory.reshape(self.heads * HD, HD), jnp.pad(normer, ((0, 16 - self.heads), (0, 0)))]
        )
        self.before = jnp.zeros_like(self.total)
        self.bits = [2**k for k in range(lax.axis_size("dp").bit_length() - 1)]
        self.sent = flip(self.total.astype(bf16), self.bits[0])

    def step(self):
        bit = self.bits.pop(0)
        received = self.order.place(self.sent).astype(f32)
        place = lax.axis_index("dp")
        mine = (place & bit) == 0 if self.later else (place & bit) != 0
        self.before = self.before + jnp.where(mine, received, 0.0)
        if self.bits:
            self.total = self.order.done(self.total + received)
            self.sent = flip(self.total.astype(bf16), self.bits[0])

    def finish(self):
        while self.bits:
            self.step()
        rows = self.heads * HD
        memory = self.before[:rows].reshape(self.heads, HD, HD)
        return memory, self.before[rows : rows + self.heads]


LIMIT = 56 * 1024 * 1024


def params():
    return pltpu.CompilerParams(vmem_limit_bytes=LIMIT)


def cost(flops, moved):
    return pl.CostEstimate(flops=flops // 64, bytes_accessed=moved // 64, transcendentals=0)


def whole_block(shape):
    return pl.BlockSpec(shape, lambda *_: (0,) * len(shape))


def dot(left_side, right_side, left_dim=1, right_dim=0, precision=None):
    return lax.dot_general(
        left_side,
        right_side,
        (((left_dim,), (right_dim,)), ((), ())),
        precision=precision,
        preferred_element_type=f32,
    )


def feature(values):
    return jnp.where(values > 0, values + 1.0, jnp.exp(jnp.minimum(values, 0.0)))


def slope(values):
    return jnp.where(values > 0, 1.0, jnp.exp(jnp.minimum(values, 0.0)))


def qkv_kernel(rows_ref, gain_ref, near_ref, far_ref, normed_ref, qkv_ref):
    half = rows_ref.shape[1] // 2

    @pl.when(pl.program_id(0) == 0)
    def _():
        rows = rows_ref[...].astype(f32)
        scale = lax.rsqrt(jnp.mean(rows * rows, axis=-1, keepdims=True) + epsilon)
        normed_ref[...] = (rows * scale * gain_ref[...]).astype(bf16)

    total = dot(normed_ref[:, :half], near_ref[...]) + dot(normed_ref[:, half:], far_ref[...])
    qkv_ref[...] = total.astype(bf16)


def norm_qkv(rows, gain, weight, columns, tile=512):
    seg, width = rows.shape
    return pl.pallas_call(
        qkv_kernel,
        grid=(columns // tile,),
        in_specs=[
            whole_block((seg, width)),
            whole_block((1, width)),
            pl.BlockSpec((width // 2, tile), lambda j: (0, j)),
            pl.BlockSpec((width // 2, tile), lambda j: (0, j)),
        ],
        out_specs=[whole_block((seg, width)), pl.BlockSpec((seg, tile), lambda j: (0, j))],
        out_shape=[
            jax.ShapeDtypeStruct((seg, width), bf16),
            jax.ShapeDtypeStruct((seg, columns), bf16),
        ],
        compiler_params=params(),
        cost_estimate=cost(2 * seg * width * columns, 2 * (2 * seg * width + (width + seg) * columns)),
    )(rows, gain[None], *weight)


def soft_rows(query, key, start):
    seg = query.shape[0]
    scores = dot(query, key, 1, 1) * float(HD) ** (-0.5)
    at_q = lax.broadcasted_iota(jnp.int32, (seg, seg), 0)
    at_k = lax.broadcasted_iota(jnp.int32, (seg, seg), 1)
    in_q = (at_q >= start) & (at_q < start + PIECE)
    in_k = (at_k >= start) & (at_k < start + PIECE)
    scores = jnp.where((at_k <= at_q) | (in_q & in_k), scores, -1e30)
    raised = jnp.exp(scores - jnp.max(scores, axis=-1, keepdims=True))
    return raised / jnp.sum(raised, axis=-1, keepdims=True)


def memory_kernel(key_ref, value_ref, memory_ref, normer_ref):
    feature_k = feature(key_ref[...].astype(f32))
    memory_ref[0] = dot(feature_k, value_ref[...].astype(f32), 0, 0, highest)
    normer_ref[0] = jnp.broadcast_to(jnp.sum(feature_k, axis=0, keepdims=True), normer_ref.shape[1:])


def local_kernel(start_ref, query_ref, key_ref, value_ref, mix_ref):
    soft = soft_rows(query_ref[...], key_ref[...], start_ref[0])
    mix_ref[...] = dot(soft.astype(bf16), value_ref[...])


def head_block(seg, heads, part):
    return pl.BlockSpec((seg, HD), lambda h: (0, part * heads + h))


def segment_memory(qkv, heads):
    seg = qkv.shape[0]
    memory, normer = pl.pallas_call(
        memory_kernel,
        grid=(heads,),
        in_specs=[head_block(seg, heads, 1), head_block(seg, heads, 2)],
        out_specs=[
            pl.BlockSpec((1, HD, HD), lambda h: (h, 0, 0)),
            pl.BlockSpec((1, 8, HD), lambda h: (h, 0, 0)),
        ],
        out_shape=[
            jax.ShapeDtypeStruct((heads, HD, HD), f32),
            jax.ShapeDtypeStruct((heads, 8, HD), f32),
        ],
        compiler_params=params(),
        cost_estimate=cost(12 * seg * heads * HD * HD, 4 * seg * heads * HD),
    )(qkv, qkv)
    return memory, normer[:, 0]


def local_attention(qkv, start, heads):
    seg = qkv.shape[0]
    return pl.pallas_call(
        local_kernel,
        grid=(heads,),
        in_specs=[pl.BlockSpec(memory_space=pltpu.SMEM)]
        + [head_block(seg, heads, part) for part in range(3)],
        out_specs=pl.BlockSpec((seg, HD), lambda h: (0, h)),
        out_shape=jax.ShapeDtypeStruct((seg, heads * HD), f32),
        compiler_params=params(),
        cost_estimate=cost(40 * seg * seg * heads * HD, 10 * seg * heads * HD),
    )(start, qkv, qkv, qkv)


def recall(query, memory, normer):
    feature_q = feature(query.astype(f32))
    denominator = jnp.sum(feature_q * normer, axis=-1, keepdims=True) + 1.0
    inverse = 1.0 / denominator
    return feature_q, inverse, dot(feature_q, memory, 1, 0, highest) * inverse


def mix_kernel(gate_ref, query_ref, mix_ref, memory_ref, normer_ref, near_ref, far_ref, heads_ref, out_ref):
    heads = memory_ref.shape[0]
    half = near_ref.shape[1]
    for h in range(heads):
        columns = slice(h * HD, (h + 1) * HD)
        gate = gate_ref[h]
        _, _, recalled = recall(query_ref[:, columns], memory_ref[h], normer_ref[h : h + 1])
        mixture = gate * recalled + (1.0 - gate) * mix_ref[:, columns]
        heads_ref[:, columns] = mixture.astype(bf16)
    out_ref[:, :half] = dot(heads_ref[...], near_ref[...]).astype(bf16)
    out_ref[:, half:] = dot(heads_ref[...], far_ref[...]).astype(bf16)


def mix_and_project(gate, qkv, local_mix, memory, normer, weight):
    seg, inner = local_mix.shape
    width = 2 * weight[0].shape[1]
    return pl.pallas_call(
        mix_kernel,
        grid=(1,),
        in_specs=[
            pl.BlockSpec(memory_space=pltpu.SMEM),
            whole_block((seg, inner)),
            whole_block((seg, inner)),
            whole_block(memory.shape),
            whole_block(normer.shape),
            whole_block(weight[0].shape),
            whole_block(weight[1].shape),
        ],
        out_specs=[whole_block((seg, inner)), whole_block((seg, width))],
        out_shape=[
            jax.ShapeDtypeStruct((seg, inner), bf16),
            jax.ShapeDtypeStruct((seg, width), bf16),
        ],
        compiler_params=params(),
        cost_estimate=cost(2 * seg * inner * (width + 6 * HD), 8 * seg * inner + 2 * (seg + inner) * width),
    )(gate, qkv, local_mix, memory, normer, *weight)


def act_kernel(
    normed_ref, cot_ref, gate_near, gate_far, up_near, up_far, down_near, down_far,
    act_ref, gate_grad_ref, up_grad_ref,
):
    half = normed_ref.shape[1] // 2
    near, far = normed_ref[:, :half], normed_ref[:, half:]
    gated = dot(near, gate_near[...]) + dot(far, gate_far[...])
    upper = dot(near, up_near[...]) + dot(far, up_far[...])
    act_grad = dot(cot_ref[:, :half], down_near[...], 1, 1) + dot(cot_ref[:, half:], down_far[...], 1, 1)
    gate = jax.nn.sigmoid(gated)
    swish = gated * gate
    act_ref[...] = (swish * upper).astype(bf16)
    gate_grad_ref[...] = (act_grad * upper * (gate * (1.0 + gated * (1.0 - gate)))).astype(bf16)
    up_grad_ref[...] = (act_grad * swish).astype(bf16)


def activations(normed, cot, gate, up, down, tile):
    seg, width = normed.shape
    hidden = down[0].shape[0]
    half = width // 2
    into = pl.BlockSpec((half, tile), lambda j: (0, j))
    back = pl.BlockSpec((tile, half), lambda j: (j, 0))
    out = pl.BlockSpec((seg, tile), lambda j: (0, j))
    return pl.pallas_call(
        act_kernel,
        grid=(hidden // tile,),
        in_specs=[whole_block((seg, width))] * 2 + [into] * 4 + [back] * 2,
        out_specs=[out] * 3,
        out_shape=[jax.ShapeDtypeStruct((seg, hidden), bf16)] * 3,
        compiler_params=params(),
        cost_estimate=cost(6 * seg * width * hidden, 6 * hidden * width + 4 * seg * width + 6 * seg * hidden),
    )(normed, cot, *gate, *up, *down)


def width_kernel(weight_dim, count, *refs):
    lefts, weights, out_ref = refs[:count], refs[count:-1], refs[-1]
    half = out_ref.shape[1] // 2
    tile = weights[0].shape[1 - weight_dim]
    for place in range(2):
        total = dot(lefts[0][...], weights[place][...], 1, weight_dim)
        for k in range(1, count):
            total = total + dot(lefts[k][...], weights[2 * k + place][...], 1, weight_dim)
        start = pl.multiple_of(place * half + pl.program_id(0) * tile, tile)
        out_ref[:, pl.ds(start, tile)] = total.astype(bf16)


def into_width(lefts, weights, weight_dim, tile=256):
    seg, inner = lefts[0].shape
    half = weights[0][0].shape[1 - weight_dim]
    shape = (inner, tile) if weight_dim == 0 else (tile, inner)
    block = pl.BlockSpec(shape, lambda j: (0, j) if weight_dim == 0 else (j, 0))
    count = len(lefts)
    return pl.pallas_call(
        functools.partial(width_kernel, weight_dim, count),
        grid=(half // tile,),
        in_specs=[whole_block((seg, inner))] * count + [block] * (2 * count),
        out_specs=whole_block((seg, 2 * half)),
        out_shape=jax.ShapeDtypeStruct((seg, 2 * half), bf16),
        compiler_params=params(),
        cost_estimate=cost(
            4 * count * seg * inner * half, count * (2 * seg * inner + 4 * inner * half) + 4 * seg * half
        ),
    )(*lefts, *[half_weight for weight in weights for half_weight in weight])


def recall_grad_kernel(
    gate_ref, keep_ref, mid_ref, near_ref, far_ref, query_ref, mix_ref, memory_ref, normer_ref,
    local_ref, query_grad_ref, memory_grad_ref, normer_grad_ref, gate_grad_ref,
):
    h = pl.program_id(0)
    half = near_ref.shape[1]
    gate = gate_ref[h]
    keep = keep_ref[0]
    mixture_grad = dot(mid_ref[:, :half], near_ref[...], 1, 1) + dot(mid_ref[:, half:], far_ref[...], 1, 1)
    normer = normer_ref[0, :1]
    feature_q, inverse, recalled = recall(query_ref[...], memory_ref[0], normer)
    gate_grad_ref[0] = jnp.broadcast_to(
        jnp.sum(mixture_grad * (recalled - mix_ref[...]), axis=0, keepdims=True), gate_grad_ref.shape[1:]
    )
    local_ref[...] = ((1.0 - gate) * mixture_grad).astype(bf16)
    share = gate * mixture_grad * inverse
    weigh = jnp.sum(share * recalled, axis=-1, keepdims=True)
    memory_grad_ref[0] = dot(feature_q, share, 0, 0, highest) * keep
    normer_grad_ref[0] = jnp.broadcast_to(
        -jnp.sum(weigh * feature_q, axis=0, keepdims=True) * keep, normer_grad_ref.shape[1:]
    )
    query_grad_ref[...] = (dot(share, memory_ref[0], 1, 1, highest) - weigh * normer) * slope(
        query_ref[...].astype(f32)
    )


def recall_backward(gate, keep, mid_seg, weight, qkv, local_mix, memory, normer):
    seg, width = mid_seg.shape
    heads = memory.shape[0]
    half = width // 2
    columns = pl.BlockSpec((seg, HD), lambda h: (0, h))
    row_block = pl.BlockSpec((1, 8, HD), lambda h: (h, 0, 0))
    memory_block = pl.BlockSpec((1, HD, HD), lambda h: (h, 0, 0))
    normer_rows = jnp.broadcast_to(normer[:, None], (heads, 8, HD))
    local_grad, query_grad, memory_grad, normer_grad, gate_grad = pl.pallas_call(
        recall_grad_kernel,
        grid=(heads,),
        in_specs=[
            pl.BlockSpec(memory_space=pltpu.SMEM),
            pl.BlockSpec(memory_space=pltpu.SMEM),
            whole_block((seg, width)),
            pl.BlockSpec((HD, half), lambda h: (h, 0)),
            pl.BlockSpec((HD, half), lambda h: (h, 0)),
            columns,
            columns,
            memory_block,
            row_block,
        ],
        out_specs=[columns, columns, memory_block, row_block, row_block],
        out_shape=[
            jax.ShapeDtypeStruct((seg, heads * HD), bf16),
            jax.ShapeDtypeStruct((seg, heads * HD), f32),
            jax.ShapeDtypeStruct((heads, HD, HD), f32),
            jax.ShapeDtypeStruct((heads, 8, HD), f32),
            jax.ShapeDtypeStruct((heads, 8, HD), f32),
        ],
        compiler_params=params(),
        cost_estimate=cost(2 * seg * heads * HD * (width + 12 * HD), 2 * seg * width + 12 * seg * heads * HD),
    )(gate, keep, mid_seg, *weight, qkv, local_mix, memory, normer_rows)
    return local_grad, query_grad, memory_grad, normer_grad[:, 0], jnp.sum(gate_grad[:, 0], axis=-1)


def local_grad_kernel(
    start_ref, query_ref, key_ref, value_ref, local_ref, extra_ref, query_grad_ref, key_grad_ref, value_grad_ref
):
    scale = float(HD) ** (-0.5)
    query, key, local = query_ref[...], key_ref[...], local_ref[...]
    soft = soft_rows(query, key, start_ref[0])
    value_grad_ref[...] = dot(soft.astype(bf16), local, 0, 0)
    prob_grad = dot(local, value_ref[...], 1, 1)
    score_grad = (soft * (prob_grad - jnp.sum(soft * prob_grad, axis=-1, keepdims=True))).astype(bf16)
    query_grad_ref[...] = (dot(score_grad, key) * scale + extra_ref[...]).astype(bf16)
    key_grad_ref[...] = dot(score_grad, query, 0, 0) * scale


def local_backward(start, qkv, local_grad, query_extra, heads):
    seg = qkv.shape[0]
    columns = pl.BlockSpec((seg, HD), lambda h: (0, h))
    return pl.pallas_call(
        local_grad_kernel,
        grid=(heads,),
        in_specs=[pl.BlockSpec(memory_space=pltpu.SMEM)]
        + [head_block(seg, heads, part) for part in range(3)]
        + [columns, columns],
        out_specs=[columns, columns, columns],
        out_shape=[
            jax.ShapeDtypeStruct((seg, heads * HD), bf16),
            jax.ShapeDtypeStruct((seg, heads * HD), f32),
            jax.ShapeDtypeStruct((seg, heads * HD), f32),
        ],
        compiler_params=params(),
        cost_estimate=cost(80 * seg * seg * heads * HD, 20 * seg * heads * HD),
    )(start, qkv, qkv, qkv, local_grad, query_extra)


def back_kernel(
    rows_ref, qkv_ref, query_grad_ref, key_grad_ref, value_grad_ref, memory_ref, normer_ref,
    near_ref, far_ref, grads_ref, part_ref, gain_ref,
):
    heads = memory_ref.shape[0]
    inner = heads * HD
    half = near_ref.shape[0]
    grads_ref[:, :inner] = query_grad_ref[...]
    for h in range(heads):
        columns = slice(h * HD, (h + 1) * HD)
        key = qkv_ref[:, inner + h * HD : inner + (h + 1) * HD].astype(f32)
        value = qkv_ref[:, 2 * inner + h * HD : 2 * inner + (h + 1) * HD].astype(f32)
        key_extra = dot(value, memory_ref[h], 1, 1, highest) + normer_ref[h : h + 1]
        grads_ref[:, inner + h * HD : inner + (h + 1) * HD] = (
            key_grad_ref[:, columns] + key_extra * slope(key)
        ).astype(bf16)
        grads_ref[:, 2 * inner + h * HD : 2 * inner + (h + 1) * HD] = (
            value_grad_ref[:, columns] + dot(feature(key), memory_ref[h], 1, 0, highest)
        ).astype(bf16)
    rows = rows_ref[...].astype(f32)
    scale = lax.rsqrt(jnp.mean(rows * rows, axis=-1, keepdims=True) + epsilon)
    for place, weight_ref in enumerate((near_ref, far_ref)):
        columns = slice(place * half, (place + 1) * half)
        part = dot(grads_ref[...], weight_ref[...], 1, 1)
        part_ref[:, columns] = part.astype(bf16)
        gain_ref[:, columns] = jnp.broadcast_to(
            jnp.sum(part * (rows[:, columns] * scale), axis=0, keepdims=True), (8, half)
        )


def attention_back(rows, qkv, query_grad, key_grad, value_grad, memory, normer, weight):
    seg, width = rows.shape
    columns = qkv.shape[1]
    inner = columns // 3
    grads, part, gain = pl.pallas_call(
        back_kernel,
        grid=(1,),
        in_specs=[
            whole_block((seg, width)),
            whole_block((seg, columns)),
            whole_block((seg, inner)),
            whole_block((seg, inner)),
            whole_block((seg, inner)),
            whole_block(memory.shape),
            whole_block(normer.shape),
            whole_block((width // 2, columns)),
            whole_block((width // 2, columns)),
        ],
        out_specs=[whole_block((seg, columns)), whole_block((seg, width)), whole_block((8, width))],
        out_shape=[
            jax.ShapeDtypeStruct((seg, columns), bf16),
            jax.ShapeDtypeStruct((seg, width), bf16),
            jax.ShapeDtypeStruct((8, width), f32),
        ],
        compiler_params=params(),
        cost_estimate=cost(2 * seg * columns * (width + 4 * HD), 2 * (width * columns + 2 * seg * width + 3 * seg * columns)),
    )(rows, qkv, query_grad, key_grad, value_grad, memory, normer, *weight)
    return grads, part, gain[0]


def grad_kernel(count, has_more, *refs):
    lefts, rights = refs[:count], refs[count : 2 * count]
    total = dot(lefts[0][...], rights[0][...], 0, 0)
    for left, right in zip(lefts[1:], rights[1:]):
        total = total + dot(left[...], right[...], 0, 0)
    if has_more:
        total = total + refs[2 * count][...].astype(f32)
    refs[-1][...] = total.astype(refs[-1].dtype)


def grad_product(lefts, rights, left_part, right_part, more=None, tile_i=256, tile_j=2048):
    seg = lefts[0].shape[0]
    height = lefts[0].shape[1] // left_part[1]
    length = rights[0].shape[1] // right_part[1]
    tile_i, tile_j = min(tile_i, height), min(tile_j, length)
    base_i, base_j = left_part[0] * (height // tile_i), right_part[0] * (length // tile_j)
    out_block = pl.BlockSpec((tile_i, tile_j), lambda i, j: (i, j))
    return pl.pallas_call(
        functools.partial(grad_kernel, len(lefts), more is not None),
        grid=(height // tile_i, length // tile_j),
        in_specs=[pl.BlockSpec((seg, tile_i), lambda i, j: (0, base_i + i)) for _ in lefts]
        + [pl.BlockSpec((seg, tile_j), lambda i, j: (0, base_j + j)) for _ in rights]
        + ([] if more is None else [out_block]),
        out_specs=out_block,
        out_shape=jax.ShapeDtypeStruct((height, length), bf16),
        compiler_params=params(),
        cost_estimate=cost(
            2 * len(lefts) * seg * height * length,
            2 * len(lefts) * seg * (height + length) + 4 * height * length,
        ),
    )(*lefts, *rights, *([] if more is None else [more]))


def inverse_rms(values):
    return lax.rsqrt(jnp.mean(values * values, axis=-1, keepdims=True) + epsilon)


def norm_pull(values, scale, gain, grad):
    weighted = gain * grad
    return scale * (
        weighted - values * (scale * scale) * jnp.mean(weighted * values, axis=-1, keepdims=True)
    )


def weight_grad(order, left_sides, right_sides, axis):
    def product(place, more=None):
        part = (place, 2)
        return grad_product(
            [order.place(left_sides[0]), *left_sides[1:]],
            right_sides,
            part if axis == 0 else (0, 1),
            part if axis == 1 else (0, 1),
            more,
        )

    return Collect(order, product, axis)


def on_device(
    hidden_in,
    out_cotangent,
    piece_start,
    query_weight,
    key_weight,
    value_weight,
    output_weight,
    gate_weight,
    up_weight,
    down_weight,
    attn_gain,
    mlp_gain,
    memory_gate,
):
    dp_index = lax.axis_index("dp")
    dp_count = lax.axis_size("dp")
    tensor_count = lax.axis_size("tensor")
    heads_here = memory_gate.shape[0]
    width = hidden_in.shape[2]
    blocks = half_order(dp_count)
    tile = 512
    order = Order()

    inward_table, outward_table = tables(dp_index, blocks)
    gate_sig = jax.nn.sigmoid(memory_gate)
    keep = jnp.where(dp_index == 0, 0.0, 1.0).astype(f32)[None]
    gain_columns = jnp.pad(jnp.stack([attn_gain, mlp_gain], axis=1), ((0, 0), (0, HD - 2)))
    qkvg = jnp.concatenate([query_weight, key_weight, value_weight, gain_columns], axis=1)
    qkv_width = qkvg.shape[1] - HD
    one = SimpleNamespace()
    two = SimpleNamespace()

    one.rows, two.rows = move_columns([hidden_in[0], hidden_in[1]], inward_table)
    order.done(one.rows)
    rows_one = OffloadGather(order, one.rows)
    rows_two = OffloadGather(order, two.rows)
    qkvg_spread = Spread(order, qkvg, 0)
    one.cot, two.cot = move_columns(
        [order.place(out_cotangent[0]), out_cotangent[1]], inward_table
    )
    order.done(one.cot)
    qkvg_spread.second()
    output_spread = Spread(order, output_weight, 1)
    qkvg_spread.third()
    one.rows_seg = rows_one.finish()

    gains = jnp.concatenate(
        [half[:, qkv_width : qkv_width + 2] for half in qkvg_spread.whole], axis=0
    )
    gains = jnp.transpose(gains.astype(f32))
    gain_one, gain_two = gains[0], gains[1]

    def project(now):
        now.seg_in, now.qkv = norm_qkv(
            order.place(now.rows_seg), gain_one, qkvg_spread.whole, qkv_width
        )
        order.done(now.qkv)

    def remember(now):
        memory, normer = segment_memory(order.place(now.qkv), heads_here)
        order.done(memory)
        now.scan = Scan(order, memory, normer, False)

    def attend(now, b):
        now.mix = local_attention(order.place(now.qkv), piece_start[b], heads_here)
        order.done(now.mix)

    def mix(now):
        now.memory, now.normer = now.scan.finish()
        now.heads_out, part = mix_and_project(
            gate_sig, order.place(now.qkv), now.mix, now.memory, now.normer,
            output_spread.whole,
        )
        order.done(now.heads_out)
        now.scatter = OffloadScatter(order, part)

    def norm_middle(now):
        now.middle = now.rows.astype(f32) + now.scatter.finish()
        now.scale_two = inverse_rms(now.middle)
        normed = (now.middle * now.scale_two * gain_two).astype(bf16)
        now.gather = OffloadGather(order, order.done(normed))

    def activate(now):
        now.act, now.gate_grad, now.up_grad = activations(
            order.place(now.seg_two), now.cot_seg, gate_spread.whole, up_spread.whole,
            down_spread.whole, tile,
        )
        order.done(now.act)

    def feed_back(now):
        part = into_width(
            [order.place(now.gate_grad), now.up_grad], [gate_spread.whole, up_spread.whole], 1
        )
        now.scatter = OffloadScatter(order, order.done(part))

    def feed_rows(now):
        part = into_width([order.place(now.act)], [down_spread.whole], 0)
        now.feed_rows = OffloadScatter(order, order.done(part))

    def norm_out(now):
        rows = now.feed_rows.finish()
        now.hidden_out = order.done((now.middle + rows).astype(bf16))

    def norm_grad(now):
        grad = now.scatter.finish()
        middle, scale = now.middle, now.scale_two
        now.gain_two_term = jnp.sum(grad * middle * scale, axis=0)
        now.middle_grad = now.cot.astype(f32) + norm_pull(middle, scale, gain_two, grad)
        now.gather = OffloadGather(order, order.done(now.middle_grad.astype(bf16)))

    def recall_back(now):
        local_grad, query_extra, memory_grad, normer_grad, now.gate_term = recall_backward(
            gate_sig, keep, order.place(now.mid_seg), output_spread.whole, now.qkv,
            now.mix, now.memory, now.normer,
        )
        now.local = order.done(local_grad), query_extra
        now.scan = Scan(order, memory_grad, normer_grad, True)

    def local_back(now, b):
        now.grads = local_backward(
            piece_start[b], order.place(now.qkv), *now.local, heads_here
        )
        order.done(now.grads[0])

    def attention_backward(now):
        now.qkv_grad, part, now.gain_one_term = attention_back(
            order.place(now.rows_seg), now.qkv, *now.grads, *now.scan.finish(),
            qkvg_spread.whole,
        )
        order.done(now.qkv_grad)
        now.scatter = OffloadScatter(order, part)

    def norm_in_grad(now):
        own_rows = now.rows.astype(f32)
        now.hidden_grad = order.done(
            now.middle_grad
            + norm_pull(own_rows, inverse_rms(own_rows), gain_one, now.scatter.finish())
        )

    def small_messages():
        gate_sum = (one.gate_term + two.gate_term) * gate_sig * (1.0 - gate_sig)
        halves_here = len(blocks)
        half_width = width // halves_here
        by_half = [term.reshape(halves_here, half_width) for term in (one.gain_one_term + two.gain_one_term, one.gain_two_term + two.gain_two_term)]
        messages = []
        for offset in range(dp_count):
            pick = [blocks.index((offset, half)) for half in range(2)]
            message = jnp.concatenate(
                [term[k] for term in by_half for k in pick] + [jnp.pad(gate_sum, (0, HD - heads_here))]
            )
            messages.append(flip(message, offset) if offset else message)
        return messages

    project(one)
    output_spread.second()
    remember(one)
    attend(one, 0)
    one.scan.step()
    output_spread.third()
    one.scan.step()
    mix(one)
    gate_spread = Spread(order, gate_weight, 0)
    two.rows_seg = rows_two.finish()
    cot_one = Gather(order, one.cot)
    project(two)
    remember(two)
    attend(two, 1)
    two.scan.step()
    cot_one.second()
    two.scan.step()
    mix(two)
    cot_one.third()
    up_spread = Spread(order, up_weight, 0)
    norm_middle(one)
    cot_two = Gather(order, two.cot)
    gate_spread.second()
    one.cot_seg = cot_one.finish()
    up_spread.second()
    cot_two.second()
    gate_spread.third()
    down_spread = Spread(order, down_weight, 1)
    cot_two.third()
    norm_middle(two)
    up_spread.third()
    down_spread.second()
    two.cot_seg = cot_two.finish()
    down_spread.third()
    one.seg_two = one.gather.finish()

    activate(one)
    feed_back(one)
    two.seg_two = two.gather.finish()
    activate(two)
    feed_back(two)
    gate_collect = weight_grad(order, [one.seg_two, two.seg_two], [one.gate_grad, two.gate_grad], 0)
    norm_grad(one)
    up_collect = weight_grad(order, [one.seg_two, two.seg_two], [one.up_grad, two.up_grad], 0)
    down_collect = weight_grad(order, [one.act, two.act], [one.cot_seg, two.cot_seg], 1)
    norm_grad(two)
    gate_collect.second()
    up_collect.second()

    one.mid_seg = one.gather.finish()
    recall_back(one)
    local_back(one, 0)
    one.scan.step()
    one.scan.step()
    attention_backward(one)
    two.mid_seg = two.gather.finish()
    recall_back(two)
    local_back(two, 1)
    two.scan.step()
    two.scan.step()
    attention_backward(two)
    feed_rows(one)
    gate_collect.third()
    down_collect.second()
    qkv_collect = weight_grad(order, [one.seg_in, two.seg_in], [one.qkv_grad, two.qkv_grad], 0)
    up_collect.third()
    feed_rows(two)
    qkv_collect.second()
    gate_total = gate_collect.finish()
    output_collect = weight_grad(order, [one.heads_out, two.heads_out], [one.mid_seg, two.mid_seg], 1)
    norm_in_grad(one)
    down_collect.third()
    output_collect.second()
    up_total = up_collect.finish()
    qkv_collect.third()
    messages = order.place(small_messages())
    norm_in_grad(two)
    down_grad = down_collect.finish()
    output_collect.third()
    norm_out(one)
    output_grad = output_collect.finish()
    norm_out(two)
    qkv_total = qkv_collect.finish()
    block = width // dp_count
    small_sum = sum(order.place(messages))
    gain_part = small_sum[: 2 * block]
    gain_sum = gain_part
    for hop in range(1, tensor_count):
        gain_sum = gain_sum + send(
            gain_part, [(i, (i + hop) % tensor_count) for i in range(tensor_count)]
        )

    query_total, key_total, value_total = cut(qkv_total, 3, 1)
    return (
        move_columns([jnp.stack([one.hidden_out, two.hidden_out])], outward_table)[0],
        move_columns([jnp.stack([one.hidden_grad, two.hidden_grad])], outward_table)[0],
        query_total,
        key_total,
        value_total,
        output_grad,
        gate_total,
        up_total,
        down_grad,
        gain_sum[:block],
        gain_sum[block:],
        small_sum[2 * block : 2 * block + heads_here],
    )


def solution(mesh):
    rows = P(None, ("dp", "tensor"))
    inward = P("dp", "tensor")
    outward = P("tensor", "dp")
    return jax.shard_map(
        on_device,
        mesh=mesh,
        in_specs=(
            rows, rows, P(None, "dp"), inward, inward, inward, outward, inward, inward, outward,
            P("dp"), P("dp"), P("tensor"),
        ),
        out_specs=(
            rows, rows, inward, inward, inward, outward, inward, inward, outward,
            P("dp"), P("dp"), P("tensor"),
        ),
        check_vma=False,
    )
```

time: 2100 us -> 777 us (0.37)
  waiting for transfers between devices: 1550 us -> 250 us
  Pallas kernels: 0 us -> 311 us
  matrix products: 304 us -> 0 us
  blocking collectives: 123 us -> 0 us
  starting transfers between devices: 2.84 us -> 74.7 us
    reduce_scatter x15 -> x8, waiting for transfers between devices: 970 us -> 22.7 us  [__init__(): lax.psum_scatter(values, 'tensor', scatter_dimension=0, tiled=True)]
    all_gather x19 -> x6, waiting for transfers between devices: 569 us -> 32.5 us  [offload_gather(): return lax.all_gather(own, 'tensor', axis=0, tiled=True)]
    pallas_call x0 -> x39, Pallas kernels: none -> 311 us  [the longest x10 81.7 us: grad_product(): pl.pallas_call(functools.partial(grad_kernel, len(lefts), more is not Non...]
    dot_general x70 -> x0, matrix products: 304 us -> none  [the longest x14 85.7 us: contract_rows(): lax.dot_general(left_side, right_side, (((0,), (0,)), ((), ())), preferre...]
    ppermute x0 -> x82, waiting for transfers between devices: none -> 195 us  [the longest x69 128 us: flip(): return lax.ppermute(values, 'dp', [(i, i ^ bit) for i in range(count)])]
    ppermute x0 -> x82, starting transfers between devices: none -> 72.8 us  [the longest x69 54 us: flip(): return lax.ppermute(values, 'dp', [(i, i ^ bit) for i in range(count)])]
    all_gather x6 -> x0, blocking collectives: 52.3 us -> none  [the longest x2 17.1 us: prefix(): gathered = jax.tree.map(lambda a: lax.all_gather(a, axis), part)]
    psum x1 -> x0, blocking collectives: 43.4 us -> none  [on_device(): gain_total, gate_total = lax.psum((gain_sums, placed), ('dp', 'tensor'))]
  transfers between devices with their start and end apart: 34 -> 96, of which waited for: 29 -> 33; matrix products, arithmetic and copies ran while one was open for 14% -> 14% of each run, Pallas kernels for 0% -> 40%
where the time goes in v1:
time: 777 us; the launch traced here: 766 us
  Pallas kernels  311 us (40%)
  waiting for transfers between devices  250 us (32%)
  starting transfers between devices  74.7 us (10%)
  other arithmetic  67.2 us (9%)
  local copies, waits for them, and re-layouts  47.5 us (6%)
  between operations  15.3 us (2%)
    ppermute x69, waiting for transfers between devices, flip(): return lax.ppermute(values, 'dp', [(i, i ^ bit) for i in range(count)])  128 us
    pallas_call x10, Pallas kernels, grad_product(): pl.pallas_call(functools.partial(grad_kernel, len(lefts), more is not Non...  81.7 us
    ppermute x13, waiting for transfers between devices, send(): return lax.ppermute(values, 'tensor', pairs)  67.3 us
    ppermute x69, starting transfers between devices, flip(): return lax.ppermute(values, 'dp', [(i, i ^ bit) for i in range(count)])  54 us
    pallas_call x4, Pallas kernels, into_width(): pl.pallas_call(functools.partial(width_kernel, weight_dim, count), grid=(...  47.9 us
    pallas_call x2, Pallas kernels, activations(): pl.pallas_call(act_kernel, grid=(hidden // tile,), in_specs=[whole_block(...  41 us
    all_gather x6, waiting for transfers between devices, offload_gather(): return lax.all_gather(own, 'tensor', axis=0, tiled=True)  32.5 us
    pallas_call x2, Pallas kernels, attention_back(): pl.pallas_call(back_kernel, grid=(1,), in_specs=[whole_block((seg, width)...  23.4 us
  transfers between devices with their start and end apart: 96, of which 33 were waited for; matrix products, arithmetic and copies ran while one was open for 14% of the time, Pallas kernels for 40%

profile of v1, /device:TPU:0, one launch (start us, length us, event | category | flops | bytes accessed | tf_op | source)
XLA Modules:
  0.0 766.3 jit_solution(10197968630130007154)
XLA Ops:
  18.2 15.2 %collective-permute-done.a_ref = bf16[256,1664]{1,0:T(8,128)(2,1)S(1)} collective-permute-done((bf16[256,1664]{1,0:T(8,128)(2,1)S(1)}, bf16[256,1664]{1,0:T(8,128)(2,1)S(1)}, u32[]{:S(2)}, u32[]{:S(2)}) %collective-permute-start) | collective-permute-done | bytes 852000 | tf_op jit(solution)/shard_map/ppermute | solution.py:52
  63.2 8.3 %shard_map.241 = (bf16[512,2048]{1,0:T(8,128)(2,1)}, bf16[512,1536]{1,0:T(8,128)(2,1)}) custom-call(bf16[512,2048]{1,0:T(8,128)(2,1)} %all-gather.7.cloned.1.call-done.rows_ref, f32[1,2048]{1,0:T(1,128)} %get-tuple-element.412.gain_ref, bf16[1024,1664]{1,0:T(8,128)(2,1)} %shard_map.240.near_ref, bf16[1024,1664]{1,0:T(8,128)(2,1)} %collective-permute-done.4.far_ref), custom_call_target="tpu_custom_call" | custom-call | flops 50331648 | bytes 188416 | tf_op jit(solution)/shard_map/pallas_call | solution.py:395
  158.4 48.3 %collective-permute-done.17 = bf16[128,2048]{1,0:T(8,128)(2,1)} collective-permute-done((bf16[128,2048]{1,0:T(8,128)(2,1)}, bf16[128,2048]{1,0:T(8,128)(2,1)}, u32[]{:S(2)}, u32[]{:S(2)}) %collective-permute-start.17) | collective-permute-done | bytes 524320 | tf_op jit(solution)/shard_map/ppermute | solution.py:223
  255.0 20.6 %collective-permute-done.32.far_1_ref = bf16[128,2048]{1,0:T(8,128)(2,1)} collective-permute-done((bf16[128,2048]{1,0:T(8,128)(2,1)}, bf16[128,2048]{1,0:T(8,128)(2,1)}, u32[]{:S(2)}, u32[]{:S(2)}) %collective-permute-start.32) | collective-permute-done | bytes 524320 | tf_op jit(solution)/shard_map/ppermute | solution.py:52
  310.6 20.7 %shard_map.253 = (bf16[512,2048]{1,0:T(8,128)(2,1)}, bf16[512,2048]{1,0:T(8,128)(2,1)}, bf16[512,2048]{1,0:T(8,128)(2,1)}) custom-call(bf16[512,2048]{1,0:T(8,128)(2,1)} %all-gather.11.cloned.1.call-done.normed_ref.refs_0_, bf16[512,2048]{1,0:T(8,128)(2,1)} %copy-done.1, bf16[1024,2048]{1,0:T(8,128)(2,1)} %shard_map.250.gate_near.refs_2_, ...), custom_call_target="tpu_custom_call" | custom-call | flops 201326592 | bytes 557056 | tf_op jit(solution)/shard_map/pallas_call | solution.py:543
  331.3 14.8 %shard_map.254 = bf16[512,2048]{1,0:T(8,128)(2,1)} custom-call(bf16[512,2048]{1,0:T(8,128)(2,1)} %get-tuple-element.261.refs_0_.refs_2_, bf16[512,2048]{1,0:T(8,128)(2,1)} %get-tuple-element.262.refs_1_.refs_2_, bf16[1024,2048]{1,0:T(8,128)(2,1)} %shard_map.250.gate_near.refs_2_, bf16[1024,2048]{1,0:T(8,128)(2,1)} %collective-permute-done.38.gate_far.refs_3_, ...), custom_call_target="tpu_custom_call" | custom-call | flops 134217728 | bytes 360448 | tf_op jit(solution)/shard_map/pallas_call | solution.py:572
  349.5 20.3 %shard_map.255 = (bf16[512,2048]{1,0:T(8,128)(2,1)}, bf16[512,2048]{1,0:T(8,128)(2,1)}, bf16[512,2048]{1,0:T(8,128)(2,1)}) custom-call(bf16[512,2048]{1,0:T(8,128)(2,1)} %all-gather.13.cloned.1.call-done.normed_ref.refs_1_, bf16[512,2048]{1,0:T(8,128)(2,1)} %copy-done, bf16[1024,2048]{1,0:T(8,128)(2,1)} %shard_map.250.gate_near.refs_2_, ...), custom_call_target="tpu_custom_call" | custom-call | flops 201326592 | bytes 557056 | tf_op jit(solution)/shard_map/pallas_call | solution.py:543
  369.8 14.8 %shard_map.256 = bf16[512,2048]{1,0:T(8,128)(2,1)} custom-call(bf16[512,2048]{1,0:T(8,128)(2,1)} %get-tuple-element.266.refs_0_.refs_3_, bf16[512,2048]{1,0:T(8,128)(2,1)} %get-tuple-element.267.refs_1_.refs_3_, bf16[1024,2048]{1,0:T(8,128)(2,1)} %shard_map.250.gate_near.refs_2_, bf16[1024,2048]{1,0:T(8,128)(2,1)} %collective-permute-done.38.gate_far.refs_3_, ...), custom_call_target="tpu_custom_call" | custom-call | flops 134217728 | bytes 360448 | tf_op jit(solution)/shard_map/pallas_call | solution.py:572
  384.7 8.8 %shard_map.257 = bf16[1024,2048]{1,0:T(8,128)(2,1)} custom-call(bf16[512,2048]{1,0:T(8,128)(2,1)} %all-gather.11.cloned.1.call-done.normed_ref.refs_0_, bf16[512,2048]{1,0:T(8,128)(2,1)} %all-gather.13.cloned.1.call-done.normed_ref.refs_1_, bf16[512,2048]{1,0:T(8,128)(2,1)} %get-tuple-element.261.refs_0_.refs_2_, ...), custom_call_target="tpu_custom_call" | custom-call | flops 67108864 | bytes 229376 | tf_op jit(solution)/shard_map/pallas_call | solution.py:757
  399.0 8.7 %shard_map.258 = bf16[1024,2048]{1,0:T(8,128)(2,1)} custom-call(bf16[512,2048]{1,0:T(8,128)(2,1)} %all-gather.11.cloned.1.call-done.normed_ref.refs_0_, bf16[512,2048]{1,0:T(8,128)(2,1)} %all-gather.13.cloned.1.call-done.normed_ref.refs_1_, bf16[512,2048]{1,0:T(8,128)(2,1)} %get-tuple-element.262.refs_1_.refs_2_, ...), custom_call_target="tpu_custom_call" | custom-call | flops 67108864 | bytes 229376 | tf_op jit(solution)/shard_map/pallas_call | solution.py:757
  408.1 10.1 %shard_map.259 = bf16[2048,1024]{1,0:T(8,128)(2,1)} custom-call(bf16[512,2048]{1,0:T(8,128)(2,1)} %get-tuple-element.308.refs_0_, bf16[512,2048]{1,0:T(8,128)(2,1)} %get-tuple-element.315.refs_1_.refs_0_, bf16[512,2048]{1,0:T(8,128)(2,1)} %copy-done.1, bf16[512,2048]{1,0:T(8,128)(2,1)} %copy-done), custom_call_target="tpu_custom_call" | custom-call | flops 67108864 | bytes 229376 | tf_op jit(solution)/shard_map/pallas_call | solution.py:757
  418.2 21.8 %reduce-scatter.13.cloned.1.call-done = bf16[128,2048]{1,0:T(8,128)(2,1)} async-done(((bf16[512,2048]{1,0:T(8,128)(2,1)}), bf16[128,2048]{1,0:T(8,128)(2,1)}) %reduce-scatter.13.cloned.1.call-update) | async-done | bytes 524304 | tf_op jit(solution)/shard_map/reduce_scatter | solution.py:253
  444.3 9.6 %shard_map.260 = bf16[1024,2048]{1,0:T(8,128)(2,1)} custom-call(bf16[512,2048]{1,0:T(8,128)(2,1)} %all-gather.11.cloned.1.call-done.normed_ref.refs_0_, bf16[512,2048]{1,0:T(8,128)(2,1)} %all-gather.13.cloned.1.call-done.normed_ref.refs_1_, bf16[512,2048]{1,0:T(8,128)(2,1)} %get-tuple-element.261.refs_0_.refs_2_, ...), custom_call_target="tpu_custom_call" | custom-call | flops 67108864 | bytes 229376 | tf_op jit(solution)/shard_map/pallas_call | solution.py:757
  453.9 9.6 %shard_map.261 = bf16[1024,2048]{1,0:T(8,128)(2,1)} custom-call(bf16[512,2048]{1,0:T(8,128)(2,1)} %all-gather.11.cloned.1.call-done.normed_ref.refs_0_, bf16[512,2048]{1,0:T(8,128)(2,1)} %all-gather.13.cloned.1.call-done.normed_ref.refs_1_, bf16[512,2048]{1,0:T(8,128)(2,1)} %get-tuple-element.262.refs_1_.refs_2_, ...), custom_call_target="tpu_custom_call" | custom-call | flops 67108864 | bytes 229376 | tf_op jit(solution)/shard_map/pallas_call | solution.py:757
  463.5 23.4 %all-gather.17.cloned.1.call-done.mid_ref.refs_2_ = bf16[512,2048]{1,0:T(8,128)(2,1)} async-done(((bf16[128,2048]{1,0:T(8,128)(2,1)}), bf16[512,2048]{1,0:T(8,128)(2,1)}) %all-gather.17.cloned.1.call-update) | async-done | bytes 2097168 | tf_op jit(solution)/shard_map/all_gather | solution.py:238
  487.5 11.3 %shard_map.262 = (bf16[512,512]{1,0:T(8,128)(2,1)}, f32[512,512]{1,0:T(8,128)}, f32[4,128,128]{2,1,0:T(8,128)}, f32[4,8,128]{2,1,0:T(8,128)}, f32[4,8,128]{2,1,0:T(8,128)}) custom-call(f32[4]{0:T(128)} %add_divide_fusion.gate_ref, f32[1]{0:T(128)} %bitcast.16.keep_ref, bf16[512,2048]{1,0:T(8,128)(2,1)} %all-gather.17.cloned.1.call-done.mid_ref.refs_2_, ...), custom_call_target="tpu_custom_call" | custom-call | flops 29360128 | bytes 81920 | tf_op jit(solution)/shard_map/pallas_call | solution.py:619
  500.6 8.3 %shard_map.263 = (bf16[512,512]{1,0:T(8,128)(2,1)}, f32[512,512]{1,0:T(8,128)}, f32[512,512]{1,0:T(8,128)}) custom-call(s32[1]{0:T(128)} %bitcast.9.start_ref, bf16[512,1536]{1,0:T(8,128)(2,1)} %get-tuple-element.281.key_ref.value_ref.query_ref.qkv_ref, bf16[512,1536]{1,0:T(8,128)(2,1)} %get-tuple-element.281.key_ref.value_ref.query_ref.qkv_ref, ...), custom_call_target="tpu_custom_call" | custom-call | flops 167772160 | bytes 81920 | tf_op jit(solution)/shard_map/pallas_call | solution.py:663
  521.7 11.7 %shard_map.264 = (bf16[512,1536]{1,0:T(8,128)(2,1)}, bf16[512,2048]{1,0:T(8,128)(2,1)}, f32[8,2048]{1,0:T(8,128)}) custom-call(bf16[512,2048]{1,0:T(8,128)(2,1)} %all-gather.7.cloned.1.call-done.rows_ref, bf16[512,1536]{1,0:T(8,128)(2,1)} %get-tuple-element.281.key_ref.value_ref.query_ref.qkv_ref, bf16[512,512]{1,0:T(8,128)(2,1)} %get-tuple-element.283.query_grad_ref, ...), custom_call_target="tpu_custom_call" | custom-call | flops 62914560 | bytes 237568 | tf_op jit(solution)/shard_map/pallas_call | solution.py:714
  534.7 11.3 %shard_map.265 = (bf16[512,512]{1,0:T(8,128)(2,1)}, f32[512,512]{1,0:T(8,128)}, f32[4,128,128]{2,1,0:T(8,128)}, f32[4,8,128]{2,1,0:T(8,128)}, f32[4,8,128]{2,1,0:T(8,128)}) custom-call(f32[4]{0:T(128)} %add_divide_fusion.gate_ref, f32[1]{0:T(128)} %bitcast.16.keep_ref, bf16[512,2048]{1,0:T(8,128)(2,1)} %all-gather.15.cloned.1.call-done.mid_ref.refs_3_, ...), custom_call_target="tpu_custom_call" | custom-call | flops 29360128 | bytes 81920 | tf_op jit(solution)/shard_map/pallas_call | solution.py:619
  568.9 11.7 %shard_map.267 = (bf16[512,1536]{1,0:T(8,128)(2,1)}, bf16[512,2048]{1,0:T(8,128)(2,1)}, f32[8,2048]{1,0:T(8,128)}) custom-call(bf16[512,2048]{1,0:T(8,128)(2,1)} %all-gather.9.cloned.1.call-done.rows_ref, bf16[512,1536]{1,0:T(8,128)(2,1)} %get-tuple-element.295.key_ref.value_ref.query_ref.qkv_ref, bf16[512,512]{1,0:T(8,128)(2,1)} %get-tuple-element.297.query_grad_ref, ...), custom_call_target="tpu_custom_call" | custom-call | flops 62914560 | bytes 237568 | tf_op jit(solution)/shard_map/pallas_call | solution.py:714
  587.3 9.1 %shard_map.268 = bf16[512,2048]{1,0:T(8,128)(2,1)} custom-call(bf16[512,2048]{1,0:T(8,128)(2,1)} %get-tuple-element.308.refs_0_, bf16[2048,1024]{1,0:T(8,128)(2,1)} %shard_map.252.down_near.refs_1_, bf16[2048,1024]{1,0:T(8,128)(2,1)} %collective-permute-done.40.down_far.refs_2_), custom_call_target="tpu_custom_call" | custom-call | flops 67108864 | bytes 196608 | tf_op jit(solution)/shard_map/pallas_call | solution.py:572
  615.0 11.0 %shard_map.269 = bf16[2048,1024]{1,0:T(8,128)(2,1)} custom-call(bf16[512,2048]{1,0:T(8,128)(2,1)} %get-tuple-element.308.refs_0_, bf16[512,2048]{1,0:T(8,128)(2,1)} %get-tuple-element.315.refs_1_.refs_0_, bf16[512,2048]{1,0:T(8,128)(2,1)} %copy-done.1, bf16[512,2048]{1,0:T(8,128)(2,1)} %copy-done, bf16[2048,1024]{1,0:T(8,128)(2,1)} %collective-permute-done.51.refs_4_), custom_call_target="tpu_custom_call" | custom-call | flops 67108864 | bytes 229376 | tf_op jit(solution)/shard_map/pallas_call | solution.py:757
  643.8 9.1 %shard_map.271 = bf16[512,2048]{1,0:T(8,128)(2,1)} custom-call(bf16[512,2048]{1,0:T(8,128)(2,1)} %get-tuple-element.315.refs_1_.refs_0_, bf16[2048,1024]{1,0:T(8,128)(2,1)} %shard_map.252.down_near.refs_1_, bf16[2048,1024]{1,0:T(8,128)(2,1)} %collective-permute-done.40.down_far.refs_2_), custom_call_target="tpu_custom_call" | custom-call | flops 67108864 | bytes 196608 | tf_op jit(solution)/shard_map/pallas_call | solution.py:572
  693.7 14.4 %collective-permute-done.64 = bf16[256,1536]{1,0:T(8,128)(2,1)S(1)} collective-permute-done((bf16[256,1536]{1,0:T(8,128)(2,1)S(1)}, bf16[256,1536]{1,0:T(8,128)(2,1)S(1)}, u32[]{:S(2)}, u32[]{:S(2)}) %collective-permute-start.64) | collective-permute-done | bytes 786464 | tf_op jit(solution)/shard_map/ppermute | solution.py:52
  (452 shorter events, 398.2 us)
Async XLA Ops:
  7.2 54.2 %all-gather.7.cloned.1.call-start = ((), (), s32[]{:S(2)}) async-start(), calls=%async_computation.8 | async-start | bytes 2621440 | tf_op jit(solution)/shard_map/all_gather | solution.py:238
  16.0 97.5 %all-gather.9.cloned.1.call-start = ((), (), s32[]{:S(2)}) async-start(), calls=%async_computation.10 | async-start | bytes 2621440 | tf_op jit(solution)/shard_map/all_gather | solution.py:238
  51.9 156.3 %reduce-scatter.9.cloned.1.call-start = ((), (), s32[]{:S(2)}) async-start(), calls=%async_computation.9 | async-start | bytes 2621440 | tf_op jit(solution)/shard_map/reduce_scatter | solution.py:253
  111.5 139.8 %reduce-scatter.11.cloned.1.call-start = ((), (), s32[]{:S(2)}) async-start(), calls=%async_computation.12 | async-start | bytes 2621440 | tf_op jit(solution)/shard_map/reduce_scatter | solution.py:253
  153.9 149.8 %all-gather.11.cloned.1.call-start = ((), (), s32[]{:S(2)}) async-start(), calls=%async_computation.11 | async-start | bytes 2621440 | tf_op jit(solution)/shard_map/all_gather | solution.py:238
  155.5 51.2 %collective-permute-start.17 = (bf16[128,2048]{1,0:T(8,128)(2,1)}, bf16[128,2048]{1,0:T(8,128)(2,1)}, u32[]{:S(2)}, u32[]{:S(2)}) collective-permute-start(bf16[128,2048]{1,0:T(8,128)(2,1)} %collective-permute-done.14), channel_id=1, source_target_pairs={{1,0},{2,3},{5,4},{6,7},{9,8},{10,11},{13,12},{14,15},{17,16},{18,... | collective-permute-start | bytes 1572872 | tf_op jit(solution)/shard_map/ppermute | solution.py:223
  156.8 55.1 %collective-permute-start.20 = (bf16[256,2048]{1,0:T(8,128)(2,1)}, bf16[256,2048]{1,0:T(8,128)(2,1)}, u32[]{:S(2)}, u32[]{:S(2)}) collective-permute-start(bf16[256,2048]{1,0:T(8,128)(2,1)} %own_ref.1), channel_id=1, source_target_pairs={{0,8},{4,12},{8,0},{12,4},{16,24},{20,28},{24,16},{28,20},{1,9},{5... | collective-permute-start | bytes 3145736 | tf_op jit(solution)/shard_map/ppermute | solution.py:52
  156.9 58.3 %collective-permute-start.21 = (bf16[256,2048]{1,0:T(8,128)(2,1)}, bf16[256,2048]{1,0:T(8,128)(2,1)}, u32[]{:S(2)}, u32[]{:S(2)}) collective-permute-start(bf16[256,2048]{1,0:T(8,128)(2,1)} %own_ref.1), channel_id=1, source_target_pairs={{0,16},{4,20},{8,24},{12,28},{16,0},{20,4},{24,8},{28,12},{1,17},{... | collective-permute-start | bytes 3145736 | tf_op jit(solution)/shard_map/ppermute | solution.py:52
  239.7 109.8 %all-gather.13.cloned.1.call-start = ((), (), s32[]{:S(2)}) async-start(), calls=%async_computation.13 | async-start | bytes 2621440 | tf_op jit(solution)/shard_map/all_gather | solution.py:238
  250.0 38.7 %collective-permute-start.37 = (bf16[128,2048]{1,0:T(8,128)(2,1)}, bf16[128,2048]{1,0:T(8,128)(2,1)}, u32[]{:S(2)}, u32[]{:S(2)}) collective-permute-start(bf16[128,2048]{1,0:T(8,128)(2,1)} %collective-permute-done.33), channel_id=1, source_target_pairs={{1,0},{2,3},{5,4},{6,7},{9,8},{10,11},{13,12},{14,15},{17,16},{18,... | collective-permute-start | bytes 1572872 | tf_op jit(solution)/shard_map/ppermute | solution.py:223
  255.0 48.8 %collective-permute-start.38 = (bf16[1024,2048]{1,0:T(8,128)(2,1)}, bf16[1024,2048]{1,0:T(8,128)(2,1)}, u32[]{:S(2)}, u32[]{:S(2)}) collective-permute-start(bf16[1024,2048]{1,0:T(8,128)(2,1)} %shard_map.250.gate_near.refs_2_), channel_id=1, source_target_pairs={{0,4},{4,0},{8,12},{12,8},{16,20},{20,16},{24,28},{28,24},{1,5},{5... | collective-permute-start | bytes 12582920 | tf_op jit(solution)/shard_map/ppermute | solution.py:52
  303.2 91.3 %reduce-scatter.15.cloned.1.call-start = ((), (), s32[]{:S(2)}) async-start(), calls=%async_computation.15 | async-start | bytes 2621440 | tf_op jit(solution)/shard_map/reduce_scatter | solution.py:253
  346.1 93.9 %reduce-scatter.13.cloned.1.call-start = ((), (), s32[]{:S(2)}) async-start(), calls=%async_computation.14 | async-start | bytes 2621440 | tf_op jit(solution)/shard_map/reduce_scatter | solution.py:253
  384.7 102.2 %all-gather.17.cloned.1.call-start = ((), (), s32[]{:S(2)}) async-start(), calls=%async_computation.17 | async-start | bytes 2621440 | tf_op jit(solution)/shard_map/all_gather | solution.py:238
  398.7 135.0 %all-gather.15.cloned.1.call-start = ((), (), s32[]{:S(2)}) async-start(), calls=%async_computation.16 | async-start | bytes 2621440 | tf_op jit(solution)/shard_map/all_gather | solution.py:238
  398.9 45.4 %collective-permute-start.41 = (bf16[1024,2048]{1,0:T(8,128)(2,1)}, bf16[1024,2048]{1,0:T(8,128)(2,1)}, u32[]{:S(2)}, u32[]{:S(2)}) collective-permute-start(bf16[1024,2048]{1,0:T(8,128)(2,1)} %shard_map.257), channel_id=1, source_target_pairs={{0,4},{4,0},{8,12},{12,8},{16,20},{20,16},{24,28},{28,24},{1,5},{5... | collective-permute-start | bytes 12582920 | tf_op jit(solution)/shard_map/ppermute | solution.py:52
  407.7 46.2 %collective-permute-start.42 = (bf16[1024,2048]{1,0:T(8,128)(2,1)}, bf16[1024,2048]{1,0:T(8,128)(2,1)}, u32[]{:S(2)}, u32[]{:S(2)}) collective-permute-start(bf16[1024,2048]{1,0:T(8,128)(2,1)} %shard_map.258), channel_id=1, source_target_pairs={{0,4},{4,0},{8,12},{12,8},{16,20},{20,16},{24,28},{28,24},{1,5},{5... | collective-permute-start | bytes 12582920 | tf_op jit(solution)/shard_map/ppermute | solution.py:52
  444.3 229.0 %reduce-scatter.19.cloned.1.call-start = ((), (), s32[]{:S(2)}) async-start(), calls=%async_computation.19 | async-start | bytes 2621440 | tf_op jit(solution)/shard_map/reduce_scatter | solution.py:253
  533.4 187.2 %reduce-scatter.21.cloned.1.call-start = ((), (), s32[]{:S(2)}) async-start(), calls=%async_computation.20 | async-start | bytes 2621440 | tf_op jit(solution)/shard_map/reduce_scatter | solution.py:253
  580.7 167.0 %reduce-scatter.17.cloned.1.call-start = ((), (), s32[]{:S(2)}) async-start(), calls=%async_computation.18 | async-start | bytes 2621440 | tf_op jit(solution)/shard_map/reduce_scatter | solution.py:253
  596.5 156.9 %reduce-scatter.23.cloned.1.call-start = ((), (), s32[]{:S(2)}) async-start(), calls=%async_computation.21 | async-start | bytes 2621440 | tf_op jit(solution)/shard_map/reduce_scatter | solution.py:253
  600.1 38.8 %collective-permute-start.56 = (bf16[256,2048]{1,0:T(8,128)(2,1)}, bf16[256,2048]{1,0:T(8,128)(2,1)S(1)}, u32[]{:S(2)}, u32[]{:S(2)}) collective-permute-start(bf16[256,2048]{1,0:T(8,128)(2,1)} %get-tuple-element.391), channel_id=1, source_target_pairs={{0,8},{4,12},{8,0},{12,4},{16,24},{20,28},{24,16},{28,20},{1,9},{5... | collective-permute-start | bytes 3145736 | tf_op jit(solution)/shard_map/ppermute | solution.py:52
  600.9 39.6 %collective-permute-start.57 = (bf16[256,2048]{1,0:T(8,128)(2,1)}, bf16[256,2048]{1,0:T(8,128)(2,1)}, u32[]{:S(2)}, u32[]{:S(2)}) collective-permute-start(bf16[256,2048]{1,0:T(8,128)(2,1)} %get-tuple-element.390), channel_id=1, source_target_pairs={{0,16},{4,20},{8,24},{12,28},{16,0},{20,4},{24,8},{28,12},{1,17},{... | collective-permute-start | bytes 3145736 | tf_op jit(solution)/shard_map/ppermute | solution.py:52
  638.9 38.9 %collective-permute-start.52 = (bf16[2048,256]{1,0:T(8,128)(2,1)}, bf16[2048,256]{1,0:T(8,128)(2,1)}, u32[]{:S(2)}, u32[]{:S(2)}) collective-permute-start(bf16[2048,256]{1,0:T(8,128)(2,1)} %get-tuple-element.383), channel_id=1, source_target_pairs={{0,8},{4,12},{8,0},{12,4},{16,24},{20,28},{24,16},{28,20},{1,9},{5... | collective-permute-start | bytes 3145736 | tf_op jit(solution)/shard_map/ppermute | solution.py:52
  (119 other events, 1570.4 us)
Sparse Core Ops, SparseCore 0:
  16.1 45.2 all-gather.6
  63.6 44.6 all-gather.8
  111.7 47.6 reduce-scatter.8
  162.2 58.8 reduce-scatter.10
  239.8 52.6 all-gather.10
  303.3 46.1 all-gather.12
  351.8 42.5 reduce-scatter.14
  396.8 43.1 reduce-scatter.12
  441.6 45.2 all-gather.16
  488.9 44.6 all-gather.14
  535.9 42.5 reduce-scatter.18
  581.3 43.1 reduce-scatter.20
  626.8 43.1 reduce-scatter.16
  672.3 43.1 reduce-scatter.22

commit v2 on v1

--- a/solution.py
+++ b/solution.py
@@ -998,6 +998,7 @@
     gate_collect.second()
     up_collect.second()
 
+    gate_collect.third()
     one.mid_seg = one.gather.finish()
     recall_back(one)
     local_back(one, 0)
@@ -1010,26 +1011,25 @@
     two.scan.step()
     two.scan.step()
     attention_backward(two)
+    qkv_collect = weight_grad(order, [one.seg_in, two.seg_in], [one.qkv_grad, two.qkv_grad], 0)
+    output_collect = weight_grad(order, [one.heads_out, two.heads_out], [one.mid_seg, two.mid_seg], 1)
+    up_collect.third()
+    qkv_collect.second()
     feed_rows(one)
-    gate_collect.third()
+    output_collect.second()
+    gate_total = gate_collect.finish()
     down_collect.second()
-    qkv_collect = weight_grad(order, [one.seg_in, two.seg_in], [one.qkv_grad, two.qkv_grad], 0)
-    up_collect.third()
     feed_rows(two)
-    qkv_collect.second()
-    gate_total = gate_collect.finish()
-    output_collect = weight_grad(order, [one.heads_out, two.heads_out], [one.mid_seg, two.mid_seg], 1)
     norm_in_grad(one)
-    down_collect.third()
-    output_collect.second()
     up_total = up_collect.finish()
     qkv_collect.third()
+    output_collect.third()
+    down_collect.third()
     messages = order.place(small_messages())
     norm_in_grad(two)
+    output_grad = output_collect.finish()
     down_grad = down_collect.finish()
-    output_collect.third()
     norm_out(one)
-    output_grad = output_collect.finish()
     norm_out(two)
     qkv_total = qkv_collect.finish()
     block = width // dp_count

time: 777 us -> 781 us (level)
    ppermute x69, waiting for transfers between devices: 128 us -> 151 us  [flip(): return lax.ppermute(values, 'dp', [(i, i ^ bit) for i in range(count)])]
    all_gather x6, waiting for transfers between devices: 32.5 us -> 9.49 us  [offload_gather(): return lax.all_gather(own, 'tensor', axis=0, tiled=True)]
  transfers between devices with their start and end apart: 96 -> 96, of which waited for: 33 -> 34; matrix products, arithmetic and copies ran while one was open for 14% -> 14% of each run, Pallas kernels for 40% -> 40%
where the time goes in v2:
time: 781 us; the launch traced here: 770 us
  Pallas kernels  311 us (40%)
  waiting for transfers between devices  252 us (32%)
  starting transfers between devices  76.9 us (10%)
  other arithmetic  68.5 us (9%)
  local copies, waits for them, and re-layouts  45.9 us (6%)
  between operations  15.7 us (2%)
    ppermute x69, waiting for transfers between devices, flip(): return lax.ppermute(values, 'dp', [(i, i ^ bit) for i in range(count)])  151 us
    pallas_call x10, Pallas kernels, grad_product(): pl.pallas_call(functools.partial(grad_kernel, len(lefts), more is not Non...  81.6 us
    ppermute x13, waiting for transfers between devices, send(): return lax.ppermute(values, 'tensor', pairs)  68 us
    ppermute x69, starting transfers between devices, flip(): return lax.ppermute(values, 'dp', [(i, i ^ bit) for i in range(count)])  56.2 us
    pallas_call x4, Pallas kernels, into_width(): pl.pallas_call(functools.partial(width_kernel, weight_dim, count), grid=(...  47.7 us
    pallas_call x2, Pallas kernels, activations(): pl.pallas_call(act_kernel, grid=(hidden // tile,), in_specs=[whole_block(...  40.9 us
    pallas_call x2, Pallas kernels, attention_back(): pl.pallas_call(back_kernel, grid=(1,), in_specs=[whole_block((seg, width)...  23.5 us
    reduce_scatter x8, waiting for transfers between devices, __init__(): lax.psum_scatter(values, 'tensor', scatter_dimension=0, tiled=True)  23.4 us
  transfers between devices with their start and end apart: 96, of which 34 were waited for; matrix products, arithmetic and copies ran while one was open for 14% of the time, Pallas kernels for 40%

profile of v2, /device:TPU:0, one launch (start us, length us, event | category | flops | bytes accessed | tf_op | source)
XLA Modules:
  0.0 770.2 jit_solution(9271970059787634998)
XLA Ops:
  18.2 15.2 %collective-permute-done.a_ref = bf16[256,1664]{1,0:T(8,128)(2,1)S(1)} collective-permute-done((bf16[256,1664]{1,0:T(8,128)(2,1)S(1)}, bf16[256,1664]{1,0:T(8,128)(2,1)S(1)}, u32[]{:S(2)}, u32[]{:S(2)}) %collective-permute-start) | collective-permute-done | bytes 852000 | tf_op jit(solution)/shard_map/ppermute | solution.py:52
  63.2 8.3 %shard_map.241 = (bf16[512,2048]{1,0:T(8,128)(2,1)}, bf16[512,1536]{1,0:T(8,128)(2,1)}) custom-call(bf16[512,2048]{1,0:T(8,128)(2,1)} %all-gather.7.cloned.1.call-done.rows_ref, f32[1,2048]{1,0:T(1,128)} %get-tuple-element.412.gain_ref, bf16[1024,1664]{1,0:T(8,128)(2,1)} %shard_map.240.near_ref, bf16[1024,1664]{1,0:T(8,128)(2,1)} %collective-permute-done.4.far_ref), custom_call_target="tpu_custom_call" | custom-call | flops 50331648 | bytes 188416 | tf_op jit(solution)/shard_map/pallas_call | solution.py:395
  158.4 48.6 %collective-permute-done.17 = bf16[128,2048]{1,0:T(8,128)(2,1)} collective-permute-done((bf16[128,2048]{1,0:T(8,128)(2,1)}, bf16[128,2048]{1,0:T(8,128)(2,1)}, u32[]{:S(2)}, u32[]{:S(2)}) %collective-permute-start.17) | collective-permute-done | bytes 524320 | tf_op jit(solution)/shard_map/ppermute | solution.py:223
  255.2 20.4 %collective-permute-done.32.far_1_ref = bf16[128,2048]{1,0:T(8,128)(2,1)} collective-permute-done((bf16[128,2048]{1,0:T(8,128)(2,1)}, bf16[128,2048]{1,0:T(8,128)(2,1)}, u32[]{:S(2)}, u32[]{:S(2)}) %collective-permute-start.32) | collective-permute-done | bytes 524320 | tf_op jit(solution)/shard_map/ppermute | solution.py:52
  310.7 20.6 %shard_map.253 = (bf16[512,2048]{1,0:T(8,128)(2,1)}, bf16[512,2048]{1,0:T(8,128)(2,1)}, bf16[512,2048]{1,0:T(8,128)(2,1)}) custom-call(bf16[512,2048]{1,0:T(8,128)(2,1)} %all-gather.11.cloned.1.call-done.normed_ref.refs_0_, bf16[512,2048]{1,0:T(8,128)(2,1)} %copy-done.1, bf16[1024,2048]{1,0:T(8,128)(2,1)} %shard_map.250.gate_near.refs_2_, ...), custom_call_target="tpu_custom_call" | custom-call | flops 201326592 | bytes 557056 | tf_op jit(solution)/shard_map/pallas_call | solution.py:543
  331.3 14.8 %shard_map.254 = bf16[512,2048]{1,0:T(8,128)(2,1)} custom-call(bf16[512,2048]{1,0:T(8,128)(2,1)} %get-tuple-element.262.refs_0_.refs_2_, bf16[512,2048]{1,0:T(8,128)(2,1)} %get-tuple-element.263.refs_1_.refs_2_, bf16[1024,2048]{1,0:T(8,128)(2,1)} %shard_map.250.gate_near.refs_2_, bf16[1024,2048]{1,0:T(8,128)(2,1)} %collective-permute-done.38.gate_far.refs_3_, ...), custom_call_target="tpu_custom_call" | custom-call | flops 134217728 | bytes 360448 | tf_op jit(solution)/shard_map/pallas_call | solution.py:572
  349.5 20.3 %shard_map.255 = (bf16[512,2048]{1,0:T(8,128)(2,1)}, bf16[512,2048]{1,0:T(8,128)(2,1)}, bf16[512,2048]{1,0:T(8,128)(2,1)}) custom-call(bf16[512,2048]{1,0:T(8,128)(2,1)} %all-gather.13.cloned.1.call-done.normed_ref.refs_1_, bf16[512,2048]{1,0:T(8,128)(2,1)} %copy-done, bf16[1024,2048]{1,0:T(8,128)(2,1)} %shard_map.250.gate_near.refs_2_, ...), custom_call_target="tpu_custom_call" | custom-call | flops 201326592 | bytes 557056 | tf_op jit(solution)/shard_map/pallas_call | solution.py:543
  369.8 14.8 %shard_map.256 = bf16[512,2048]{1,0:T(8,128)(2,1)} custom-call(bf16[512,2048]{1,0:T(8,128)(2,1)} %get-tuple-element.267.refs_0_.refs_3_, bf16[512,2048]{1,0:T(8,128)(2,1)} %get-tuple-element.268.refs_1_.refs_3_, bf16[1024,2048]{1,0:T(8,128)(2,1)} %shard_map.250.gate_near.refs_2_, bf16[1024,2048]{1,0:T(8,128)(2,1)} %collective-permute-done.38.gate_far.refs_3_, ...), custom_call_target="tpu_custom_call" | custom-call | flops 134217728 | bytes 360448 | tf_op jit(solution)/shard_map/pallas_call | solution.py:572
  384.7 8.8 %shard_map.257 = bf16[1024,2048]{1,0:T(8,128)(2,1)} custom-call(bf16[512,2048]{1,0:T(8,128)(2,1)} %all-gather.11.cloned.1.call-done.normed_ref.refs_0_, bf16[512,2048]{1,0:T(8,128)(2,1)} %all-gather.13.cloned.1.call-done.normed_ref.refs_1_, bf16[512,2048]{1,0:T(8,128)(2,1)} %get-tuple-element.262.refs_0_.refs_2_, ...), custom_call_target="tpu_custom_call" | custom-call | flops 67108864 | bytes 229376 | tf_op jit(solution)/shard_map/pallas_call | solution.py:757
  398.7 8.7 %shard_map.258 = bf16[1024,2048]{1,0:T(8,128)(2,1)} custom-call(bf16[512,2048]{1,0:T(8,128)(2,1)} %all-gather.11.cloned.1.call-done.normed_ref.refs_0_, bf16[512,2048]{1,0:T(8,128)(2,1)} %all-gather.13.cloned.1.call-done.normed_ref.refs_1_, bf16[512,2048]{1,0:T(8,128)(2,1)} %get-tuple-element.263.refs_1_.refs_2_, ...), custom_call_target="tpu_custom_call" | custom-call | flops 67108864 | bytes 229376 | tf_op jit(solution)/shard_map/pallas_call | solution.py:757
  407.4 10.1 %shard_map.259 = bf16[2048,1024]{1,0:T(8,128)(2,1)} custom-call(bf16[512,2048]{1,0:T(8,128)(2,1)} %get-tuple-element.318.refs_0_, bf16[512,2048]{1,0:T(8,128)(2,1)} %get-tuple-element.320.refs_1_.refs_0_, bf16[512,2048]{1,0:T(8,128)(2,1)} %copy-done.1, bf16[512,2048]{1,0:T(8,128)(2,1)} %copy-done), custom_call_target="tpu_custom_call" | custom-call | flops 67108864 | bytes 229376 | tf_op jit(solution)/shard_map/pallas_call | solution.py:757
  417.5 22.5 %reduce-scatter.13.cloned.1.call-done = bf16[128,2048]{1,0:T(8,128)(2,1)} async-done(((bf16[512,2048]{1,0:T(8,128)(2,1)}), bf16[128,2048]{1,0:T(8,128)(2,1)}) %reduce-scatter.13.cloned.1.call-update) | async-done | bytes 524304 | tf_op jit(solution)/shard_map/reduce_scatter | solution.py:253
  444.5 9.6 %shard_map.260 = bf16[1024,2048]{1,0:T(8,128)(2,1)} custom-call(bf16[512,2048]{1,0:T(8,128)(2,1)} %all-gather.11.cloned.1.call-done.normed_ref.refs_0_, bf16[512,2048]{1,0:T(8,128)(2,1)} %all-gather.13.cloned.1.call-done.normed_ref.refs_1_, bf16[512,2048]{1,0:T(8,128)(2,1)} %get-tuple-element.262.refs_0_.refs_2_, ...), custom_call_target="tpu_custom_call" | custom-call | flops 67108864 | bytes 229376 | tf_op jit(solution)/shard_map/pallas_call | solution.py:757
  460.1 9.5 %shard_map.261 = bf16[1024,2048]{1,0:T(8,128)(2,1)} custom-call(bf16[512,2048]{1,0:T(8,128)(2,1)} %all-gather.11.cloned.1.call-done.normed_ref.refs_0_, bf16[512,2048]{1,0:T(8,128)(2,1)} %all-gather.13.cloned.1.call-done.normed_ref.refs_1_, bf16[512,2048]{1,0:T(8,128)(2,1)} %get-tuple-element.263.refs_1_.refs_2_, ...), custom_call_target="tpu_custom_call" | custom-call | flops 67108864 | bytes 229376 | tf_op jit(solution)/shard_map/pallas_call | solution.py:757
  469.7 12.4 %collective-permute-done.45 = bf16[256,2048]{1,0:T(8,128)(2,1)S(1)} collective-permute-done((bf16[256,2048]{1,0:T(8,128)(2,1)}, bf16[256,2048]{1,0:T(8,128)(2,1)S(1)}, u32[]{:S(2)}, u32[]{:S(2)}) %collective-permute-start.45) | collective-permute-done | bytes 1048608 | tf_op jit(solution)/shard_map/ppermute | solution.py:52
  487.2 11.3 %shard_map.262 = (bf16[512,512]{1,0:T(8,128)(2,1)}, f32[512,512]{1,0:T(8,128)}, f32[4,128,128]{2,1,0:T(8,128)}, f32[4,8,128]{2,1,0:T(8,128)}, f32[4,8,128]{2,1,0:T(8,128)}) custom-call(f32[4]{0:T(128)} %add_divide_fusion.gate_ref, f32[1]{0:T(128)} %bitcast.16.keep_ref, bf16[512,2048]{1,0:T(8,128)(2,1)} %all-gather.17.cloned.1.call-done.mid_ref.refs_2_, ...), custom_call_target="tpu_custom_call" | custom-call | flops 29360128 | bytes 81920 | tf_op jit(solution)/shard_map/pallas_call | solution.py:619
  523.2 11.7 %shard_map.264 = (bf16[512,1536]{1,0:T(8,128)(2,1)}, bf16[512,2048]{1,0:T(8,128)(2,1)}, f32[8,2048]{1,0:T(8,128)}) custom-call(bf16[512,2048]{1,0:T(8,128)(2,1)} %all-gather.7.cloned.1.call-done.rows_ref, bf16[512,1536]{1,0:T(8,128)(2,1)} %get-tuple-element.284.key_ref.value_ref.query_ref.qkv_ref, bf16[512,512]{1,0:T(8,128)(2,1)} %get-tuple-element.286.query_grad_ref, ...), custom_call_target="tpu_custom_call" | custom-call | flops 62914560 | bytes 237568 | tf_op jit(solution)/shard_map/pallas_call | solution.py:714
  536.2 11.3 %shard_map.265 = (bf16[512,512]{1,0:T(8,128)(2,1)}, f32[512,512]{1,0:T(8,128)}, f32[4,128,128]{2,1,0:T(8,128)}, f32[4,8,128]{2,1,0:T(8,128)}, f32[4,8,128]{2,1,0:T(8,128)}) custom-call(f32[4]{0:T(128)} %add_divide_fusion.gate_ref, f32[1]{0:T(128)} %bitcast.16.keep_ref, bf16[512,2048]{1,0:T(8,128)(2,1)} %all-gather.15.cloned.1.call-done.mid_ref.refs_3_, ...), custom_call_target="tpu_custom_call" | custom-call | flops 29360128 | bytes 81920 | tf_op jit(solution)/shard_map/pallas_call | solution.py:619
  570.3 11.8 %shard_map.267 = (bf16[512,1536]{1,0:T(8,128)(2,1)}, bf16[512,2048]{1,0:T(8,128)(2,1)}, f32[8,2048]{1,0:T(8,128)}) custom-call(bf16[512,2048]{1,0:T(8,128)(2,1)} %all-gather.9.cloned.1.call-done.rows_ref, bf16[512,1536]{1,0:T(8,128)(2,1)} %get-tuple-element.298.key_ref.value_ref.query_ref.qkv_ref, bf16[512,512]{1,0:T(8,128)(2,1)} %get-tuple-element.300.query_grad_ref, ...), custom_call_target="tpu_custom_call" | custom-call | flops 62914560 | bytes 237568 | tf_op jit(solution)/shard_map/pallas_call | solution.py:714
  600.9 16.9 %collective-permute-done.43 = bf16[256,2048]{1,0:T(8,128)(2,1)} collective-permute-done((bf16[256,2048]{1,0:T(8,128)(2,1)}, bf16[256,2048]{1,0:T(8,128)(2,1)}, u32[]{:S(2)}, u32[]{:S(2)}) %collective-permute-start.43) | collective-permute-done | bytes 1048608 | tf_op jit(solution)/shard_map/ppermute | solution.py:52
  630.4 9.1 %shard_map.271 = bf16[512,2048]{1,0:T(8,128)(2,1)} custom-call(bf16[512,2048]{1,0:T(8,128)(2,1)} %get-tuple-element.318.refs_0_, bf16[2048,1024]{1,0:T(8,128)(2,1)} %shard_map.252.down_near.refs_1_, bf16[2048,1024]{1,0:T(8,128)(2,1)} %collective-permute-done.40.down_far.refs_2_), custom_call_target="tpu_custom_call" | custom-call | flops 67108864 | bytes 196608 | tf_op jit(solution)/shard_map/pallas_call | solution.py:572
  653.4 11.1 %shard_map.273 = bf16[2048,1024]{1,0:T(8,128)(2,1)} custom-call(bf16[512,2048]{1,0:T(8,128)(2,1)} %get-tuple-element.318.refs_0_, bf16[512,2048]{1,0:T(8,128)(2,1)} %get-tuple-element.320.refs_1_.refs_0_, bf16[512,2048]{1,0:T(8,128)(2,1)} %copy-done.1, bf16[512,2048]{1,0:T(8,128)(2,1)} %copy-done, bf16[2048,1024]{1,0:T(8,128)(2,1)} %collective-permute-done.57.refs_4_), custom_call_target="tpu_custom_call" | custom-call | flops 67108864 | bytes 229376 | tf_op jit(solution)/shard_map/pallas_call | solution.py:757
  668.1 9.1 %shard_map.274 = bf16[512,2048]{1,0:T(8,128)(2,1)} custom-call(bf16[512,2048]{1,0:T(8,128)(2,1)} %get-tuple-element.320.refs_1_.refs_0_, bf16[2048,1024]{1,0:T(8,128)(2,1)} %shard_map.252.down_near.refs_1_, bf16[2048,1024]{1,0:T(8,128)(2,1)} %collective-permute-done.40.down_far.refs_2_), custom_call_target="tpu_custom_call" | custom-call | flops 67108864 | bytes 196608 | tf_op jit(solution)/shard_map/pallas_call | solution.py:572
  697.1 19.4 %collective-permute-done.60 = bf16[512,256]{1,0:T(8,128)(2,1)S(1)} collective-permute-done((bf16[512,256]{1,0:T(8,128)(2,1)S(1)}, bf16[512,256]{1,0:T(8,128)(2,1)S(1)}, u32[]{:S(2)}, u32[]{:S(2)}) %collective-permute-start.60) | collective-permute-done | bytes 262176 | tf_op jit(solution)/shard_map/ppermute | solution.py:52
  (462 shorter events, 398.4 us)
Async XLA Ops:
  7.2 54.2 %all-gather.7.cloned.1.call-start = ((), (), s32[]{:S(2)}) async-start(), calls=%async_computation.8 | async-start | bytes 2621440 | tf_op jit(solution)/shard_map/all_gather | solution.py:238
  16.0 97.4 %all-gather.9.cloned.1.call-start = ((), (), s32[]{:S(2)}) async-start(), calls=%async_computation.10 | async-start | bytes 2621440 | tf_op jit(solution)/shard_map/all_gather | solution.py:238
  51.9 156.6 %reduce-scatter.9.cloned.1.call-start = ((), (), s32[]{:S(2)}) async-start(), calls=%async_computation.9 | async-start | bytes 2621440 | tf_op jit(solution)/shard_map/reduce_scatter | solution.py:253
  111.6 140.0 %reduce-scatter.11.cloned.1.call-start = ((), (), s32[]{:S(2)}) async-start(), calls=%async_computation.12 | async-start | bytes 2621440 | tf_op jit(solution)/shard_map/reduce_scatter | solution.py:253
  154.0 149.7 %all-gather.11.cloned.1.call-start = ((), (), s32[]{:S(2)}) async-start(), calls=%async_computation.11 | async-start | bytes 2621440 | tf_op jit(solution)/shard_map/all_gather | solution.py:238
  155.5 51.4 %collective-permute-start.17 = (bf16[128,2048]{1,0:T(8,128)(2,1)}, bf16[128,2048]{1,0:T(8,128)(2,1)}, u32[]{:S(2)}, u32[]{:S(2)}) collective-permute-start(bf16[128,2048]{1,0:T(8,128)(2,1)} %collective-permute-done.14), channel_id=1, source_target_pairs={{1,0},{2,3},{5,4},{6,7},{9,8},{10,11},{13,12},{14,15},{17,16},{18,... | collective-permute-start | bytes 1572872 | tf_op jit(solution)/shard_map/ppermute | solution.py:223
  156.9 55.3 %collective-permute-start.20 = (bf16[256,2048]{1,0:T(8,128)(2,1)}, bf16[256,2048]{1,0:T(8,128)(2,1)}, u32[]{:S(2)}, u32[]{:S(2)}) collective-permute-start(bf16[256,2048]{1,0:T(8,128)(2,1)} %own_ref.1), channel_id=1, source_target_pairs={{0,8},{4,12},{8,0},{12,4},{16,24},{20,28},{24,16},{28,20},{1,9},{5... | collective-permute-start | bytes 3145736 | tf_op jit(solution)/shard_map/ppermute | solution.py:52
  156.9 58.5 %collective-permute-start.21 = (bf16[256,2048]{1,0:T(8,128)(2,1)}, bf16[256,2048]{1,0:T(8,128)(2,1)}, u32[]{:S(2)}, u32[]{:S(2)}) collective-permute-start(bf16[256,2048]{1,0:T(8,128)(2,1)} %own_ref.1), channel_id=1, source_target_pairs={{0,16},{4,20},{8,24},{12,28},{16,0},{20,4},{24,8},{28,12},{1,17},{... | collective-permute-start | bytes 3145736 | tf_op jit(solution)/shard_map/ppermute | solution.py:52
  239.9 109.6 %all-gather.13.cloned.1.call-start = ((), (), s32[]{:S(2)}) async-start(), calls=%async_computation.13 | async-start | bytes 2621440 | tf_op jit(solution)/shard_map/all_gather | solution.py:238
  255.2 48.5 %collective-permute-start.38 = (bf16[1024,2048]{1,0:T(8,128)(2,1)}, bf16[1024,2048]{1,0:T(8,128)(2,1)}, u32[]{:S(2)}, u32[]{:S(2)}) collective-permute-start(bf16[1024,2048]{1,0:T(8,128)(2,1)} %shard_map.250.gate_near.refs_2_), channel_id=1, source_target_pairs={{0,4},{4,0},{8,12},{12,8},{16,20},{20,16},{24,28},{28,24},{1,5},{5... | collective-permute-start | bytes 12582920 | tf_op jit(solution)/shard_map/ppermute | solution.py:52
  303.2 91.1 %reduce-scatter.15.cloned.1.call-start = ((), (), s32[]{:S(2)}) async-start(), calls=%async_computation.15 | async-start | bytes 2621440 | tf_op jit(solution)/shard_map/reduce_scatter | solution.py:253
  346.1 93.8 %reduce-scatter.13.cloned.1.call-start = ((), (), s32[]{:S(2)}) async-start(), calls=%async_computation.14 | async-start | bytes 2621440 | tf_op jit(solution)/shard_map/reduce_scatter | solution.py:253
  384.6 102.0 %all-gather.17.cloned.1.call-start = ((), (), s32[]{:S(2)}) async-start(), calls=%async_computation.17 | async-start | bytes 2621440 | tf_op jit(solution)/shard_map/all_gather | solution.py:238
  393.5 51.0 %collective-permute-start.41 = (bf16[1024,2048]{1,0:T(8,128)(2,1)}, bf16[1024,2048]{1,0:T(8,128)(2,1)}, u32[]{:S(2)}, u32[]{:S(2)}) collective-permute-start(bf16[1024,2048]{1,0:T(8,128)(2,1)} %shard_map.257), channel_id=1, source_target_pairs={{0,4},{4,0},{8,12},{12,8},{16,20},{20,16},{24,28},{28,24},{1,5},{5... | collective-permute-start | bytes 12582920 | tf_op jit(solution)/shard_map/ppermute | solution.py:52
  398.6 136.6 %all-gather.15.cloned.1.call-start = ((), (), s32[]{:S(2)}) async-start(), calls=%async_computation.16 | async-start | bytes 2621440 | tf_op jit(solution)/shard_map/all_gather | solution.py:238
  407.4 52.7 %collective-permute-start.42 = (bf16[1024,2048]{1,0:T(8,128)(2,1)}, bf16[1024,2048]{1,0:T(8,128)(2,1)}, u32[]{:S(2)}, u32[]{:S(2)}) collective-permute-start(bf16[1024,2048]{1,0:T(8,128)(2,1)} %shard_map.258), channel_id=1, source_target_pairs={{0,4},{4,0},{8,12},{12,8},{16,20},{20,16},{24,28},{28,24},{1,5},{5... | collective-permute-start | bytes 12582920 | tf_op jit(solution)/shard_map/ppermute | solution.py:52
  444.2 236.8 %reduce-scatter.19.cloned.1.call-start = ((), (), s32[]{:S(2)}) async-start(), calls=%async_computation.19 | async-start | bytes 2621440 | tf_op jit(solution)/shard_map/reduce_scatter | solution.py:253
  535.0 196.8 %reduce-scatter.21.cloned.1.call-start = ((), (), s32[]{:S(2)}) async-start(), calls=%async_computation.20 | async-start | bytes 2621440 | tf_op jit(solution)/shard_map/reduce_scatter | solution.py:253
  582.1 172.7 %reduce-scatter.17.cloned.1.call-start = ((), (), s32[]{:S(2)}) async-start(), calls=%async_computation.18 | async-start | bytes 2621440 | tf_op jit(solution)/shard_map/reduce_scatter | solution.py:253
  595.4 58.0 %collective-permute-start.57 = (bf16[2048,1024]{1,0:T(8,128)(2,1)}, bf16[2048,1024]{1,0:T(8,128)(2,1)}, u32[]{:S(2)}, u32[]{:S(2)}) collective-permute-start(bf16[2048,1024]{1,0:T(8,128)(2,1)} %shard_map.259), channel_id=1, source_target_pairs={{0,4},{4,0},{8,12},{12,8},{16,20},{20,16},{24,28},{28,24},{1,5},{5... | collective-permute-start | bytes 12582920 | tf_op jit(solution)/shard_map/ppermute | solution.py:52
  595.4 53.6 %collective-permute-start.54 = (bf16[128,2048]{1,0:T(8,128)(2,1)}, bf16[128,2048]{1,0:T(8,128)(2,1)}, u32[]{:S(2)}, u32[]{:S(2)}) collective-permute-start(bf16[128,2048]{1,0:T(8,128)(2,1)} %get-tuple-element.389), channel_id=1, source_target_pairs={{0,8},{4,12},{8,0},{12,4},{16,24},{20,28},{24,16},{28,20},{1,9},{5... | collective-permute-start | bytes 1572872 | tf_op jit(solution)/shard_map/ppermute | solution.py:52
  639.5 116.8 %reduce-scatter.23.cloned.1.call-start = ((), (), s32[]{:S(2)}) async-start(), calls=%async_computation.21 | async-start | bytes 2621440 | tf_op jit(solution)/shard_map/reduce_scatter | solution.py:253
  641.5 80.1 %collective-permute-start.72 = (f32[640]{0:T(1024)S(1)}, f32[640]{0:T(1024)S(1)}, u32[]{:S(2)}, u32[]{:S(2)}) collective-permute-start(f32[640]{0:T(1024)S(1)} %get-tuple-element.441), channel_id=1, source_target_pairs={{0,4},{4,0},{8,12},{12,8},{16,20},{20,16},{24,28},{28,24},{1,5},{5... | collective-permute-start | bytes 7688 | tf_op jit(solution)/shard_map/ppermute | solution.py:52
  643.3 43.1 %collective-permute-start.64 = (bf16[128,2048]{1,0:T(8,128)(2,1)}, bf16[128,2048]{1,0:T(8,128)(2,1)}, u32[]{:S(2)}, u32[]{:S(2)}) collective-permute-start(bf16[128,2048]{1,0:T(8,128)(2,1)} %get-tuple-element.385), channel_id=1, source_target_pairs={{0,8},{4,12},{8,0},{12,4},{16,24},{20,28},{24,16},{28,20},{1,9},{5... | collective-permute-start | bytes 1572872 | tf_op jit(solution)/shard_map/ppermute | solution.py:52
  (124 other events, 1570.5 us)
Sparse Core Ops, SparseCore 0:
  16.1 45.2 all-gather.6
  63.6 44.6 all-gather.8
  111.7 47.6 reduce-scatter.8
  162.2 58.9 reduce-scatter.10
  240.0 52.5 all-gather.10
  303.4 46.0 all-gather.12
  351.8 42.5 reduce-scatter.14
  396.8 43.1 reduce-scatter.12
  441.6 45.0 all-gather.16
  488.6 44.8 all-gather.14
  535.8 42.5 reduce-scatter.18
  582.2 42.6 reduce-scatter.20
  639.6 41.6 reduce-scatter.16
  683.6 43.1 reduce-scatter.22
